TPU v7x, 32 devices: a whole 2x2x4 slice. The times are simulated.
32 devices in a mesh: tile: 8 (over y, x, core), depth: 4 (over z).
Axes of the slice: x: 2, y: 2, z: 4, core: 2. Of those that a mesh axis runs over, the one named last changes fastest.
Arguments:
- coefficients: float32 [8, 4, 8, 32, 128], P(None, 'depth', 'tile'), may hold values from -24 to 24
- keep_count: int32 [4, 8, 32, 128], P('depth', 'tile'), may hold values from 1 to 8, as said below
- view_flip: int32 [8], P('tile'), may hold values from 0 to 1
Outputs:
- image: float32 [4, 128, 512], P(None, 'tile', 'depth')
Inputs may be any that keep to these rules, and one draw needn't show every extreme that they name: `keep_count`: along the block rows, blocks 2 j and 2 j + 1 of every brick and block column retain 8 + 1 slots together.
All inputs are finite; a program needn't handle non-finite values.
Results may differ from a plain program's by a relative error of at most 0.0003.
Values sent between devices are 32-bit elements; how exact they have to be, the bound alone decides.
No kernel may reach another device: no remote copies, remote signals or barrier semaphores. Data moves between devices by JAX's collectives and lax.ppermute only.
A program may use at most 64 MiB of HBM per device.

v0:
```python
import math

import jax
import jax.numpy as jnp
from jax import lax
from jax.experimental import pallas as pl
from jax.experimental.pallas import tpu as pltpu
from jax.sharding import PartitionSpec as P

LOG2E = math.log2(math.e)
EDGE = 4


def cosine(frequency, position):
    factor = 0.5 if frequency == 0 else math.sqrt(0.5)
    return factor * math.cos(math.pi * (2 * position + 1) * frequency / 8.0)


def swap_halves(values):
    half = values.shape[1] // 2
    if values.shape[1] % 128 == 0:
        return pltpu.roll(values, half, 1)
    return jnp.concatenate([values[:, half:], values[:, :half]], axis=1)


def pack_kernel(
    flip_ref, coef_hbm, keep_hbm, out_ref, sign_ref, coef_ref, keep_ref, arrival, *, tiles, depths
):
    _, columns, rows = coef_ref.shape
    strip = columns // tiles
    band = rows // depths
    moves = ((coef_hbm, coef_ref), (keep_hbm, keep_ref))
    fetches = [pltpu.make_async_copy(a, b, arrival.at[i]) for i, (a, b) in enumerate(moves)]
    for fetch in fetches:
        fetch.start()
    for fetch in fetches:
        fetch.wait()
    lane = lax.broadcasted_iota(jnp.int32, (tiles, rows), 1)
    even = lane % 2 == 0

    def take(values, index):
        return jnp.take_along_axis(values, index, axis=1)

    other = lane + 1 - 2 * (lane % 2)
    packed = []
    for b in range(strip):
        mine = pl.ds(b, tiles, stride=strip)
        keep = keep_ref[mine, :]
        slot = [coef_ref[k, mine, :] for k in range(8)]
        result = [slot[0]]
        for q in (1, 2, 3, 4):
            result.append(jnp.where(keep > q, slot[q], take(slot[8 - q], other)))
        result[4] = jnp.where(even, result[4], (9 - keep).astype(jnp.float32))
        packed.append(result)
    sign_ref[...] = jnp.full(sign_ref.shape, 1 - 2 * flip_ref[0], jnp.int32).astype(jnp.float32)
    half = strip * band // 2
    parity = lane // half % 2
    column = lane // (band // 2) % strip
    source = lane % (band // 2) * 2 + parity
    for d in range(depths):
        for q in range(5):
            gathered = [take(packed[b][q], source + d * band) for b in range(strip)]
            merged = gathered[0]
            for b in range(1, strip):
                merged = jnp.where(column == b, gathered[b], merged)
            out_ref[:, d, q, 0, :] = merged[:, : 2 * half]


def unpack(packed_ref, coef_ref):
    tiles, depths, _, _, lanes = packed_ref.shape
    zblocks = tiles * depths
    first = lax.broadcasted_iota(jnp.int32, (zblocks, lanes), 1) < lanes // 2
    row = [packed_ref[:, :, q, 0, :].reshape(zblocks, lanes) for q in range(5)]
    turned = [None] + [swap_halves(row[q]) for q in (1, 2, 3, 4)]
    keep = jnp.where(first, turned[4], 9.0 - row[4])
    slot = [row[0]] + [jnp.where(keep > q, row[q], 0.0) for q in (1, 2, 3)]
    slot.append(jnp.where(keep > 4, jnp.where(first, row[4], turned[4]), 0.0))
    slot += [jnp.where(keep > k, turned[8 - k], 0.0) for k in (5, 6, 7)]
    for k in range(8):
        coef_ref[k] = slot[k]


def render_kernel(sign_ref, packed_ref, out_ref, coef_ref, *, strip, band, samples):
    unpack(packed_ref, coef_ref)
    slots, zblocks, lanes = coef_ref.shape
    tiles, depths = packed_ref.shape[:2]
    sign = sign_ref[...]
    flipped = jnp.max(sign) < 0.0
    b1 = [cosine(1, i) for i in range(EDGE)]
    row = lax.broadcasted_iota(jnp.int32, (2 * EDGE, lanes), 0)
    x = row % EDGE
    y = row // EDGE

    def table(position, values):
        result = jnp.full((2 * EDGE, lanes), values[0], jnp.float32)
        for i in range(1, len(values)):
            result = jnp.where(position == i, jnp.float32(values[i]), result)
        return result

    x1 = table(x, b1)
    x2 = table(x, [cosine(2, i) for i in range(EDGE)])
    y1 = table(y, b1[:2])
    y2 = table(y, [cosine(2, i) for i in range(2)])
    c_dc = 0.125 * LOG2E
    c_x1 = (0.25 * LOG2E) * x1
    c_x2 = (0.25 * LOG2E) * x2
    c_y1 = (0.25 * LOG2E) * y1
    c_y2 = (0.25 * LOG2E) * y2
    c_xy = (0.5 * LOG2E) * x1 * y1
    c_z = jnp.full((2 * EDGE, lanes), 0.25 * LOG2E * b1[0], jnp.float32) * sign
    c_zy = (0.5 * LOG2E * b1[0]) * y1 * sign
    ratio = b1[1] / b1[0]
    blue_factor = math.exp(-1.5)
    fade = -1.5 / samples

    def block(step, state):
        source = jnp.where(flipped, zblocks - 1 - step, step)
        zb = source % tiles * depths + source // tiles
        a = [
            jnp.broadcast_to(coef_ref[k, pl.ds(zb, 1), :], (2 * EDGE, lanes)) for k in range(slots)
        ]
        even = a[0] * c_dc + a[2] * c_x1 + a[4] * c_y2 + a[6] * c_x2
        odd = a[1] * c_y1 + a[5] * c_xy
        g_even = a[3] * c_z
        g_odd = a[7] * c_zy
        halves = []
        for h in range(2):
            depth, before, red, green, blue = state[h]
            base = even + odd if h == 0 else even - odd
            g = g_even + g_odd if h == 0 else g_even - g_odd
            near = g * ratio
            for f in (base + g, base + near, base - near, base - g):
                v = jnp.exp2(f)
                one_u = 1.0 + v * v
                depth = depth + jnp.log2(one_u)
                after = jnp.exp2(fade * depth)
                weight = before - after
                before = after
                red = red + weight / one_u
                green = green + weight * jnp.exp2(f * (f * (-1.0 / LOG2E)))
                blue = blue + weight / (1.0 + blue_factor * v)
            halves.append((depth, before, red, green, blue))
        return tuple(halves)

    zero = jnp.zeros((2 * EDGE, lanes), jnp.float32)
    one = jnp.ones((2 * EDGE, lanes), jnp.float32)
    start = (zero, one, zero, zero, zero)
    state = lax.fori_loop(0, zblocks, block, (start, start), unroll=4)

    width = band * EDGE
    pick = lax.broadcasted_iota(jnp.int32, (2 * EDGE, width), 1)
    y_out = pick % EDGE
    place = pick // EDGE
    place = place % 2 * (lanes // 2) + place // 2
    outs = []
    for _, before, red, green, blue in state:
        opacity = 1.0 - before
        outs.append((opacity - red, green, blue, opacity))
    for ch in range(4):
        for b in range(strip):
            index = place + b * (band // 2)
            low = jnp.take_along_axis(outs[0][ch], index, axis=1)
            high = jnp.take_along_axis(outs[1][ch], index, axis=1)
            both = jnp.where(y_out < 2, low, high)
            first, second = both[:EDGE], both[EDGE:]
            use_first = (y_out[:EDGE] == 0) | (y_out[:EDGE] == 3)
            out_ref[ch, pl.ds(b * EDGE, EDGE), :] = jnp.where(use_first, first, second)


def per_device(coefficients, keep_count, view_flip):
    tiles = lax.axis_size("tile")
    depths = lax.axis_size("depth")
    slots, _, _, columns, rows = coefficients.shape
    strip = columns // tiles
    band = rows // depths
    zblocks = tiles * depths
    vmem = pl.BlockSpec(memory_space=pltpu.VMEM)
    params = pltpu.CompilerParams(vmem_limit_bytes=8 * 1024 * 1024)
    lanes = strip * band
    inputs = (coefficients.reshape(slots, columns, rows), keep_count.reshape(columns, rows))
    outgoing, sign = pl.pallas_call(
        lambda *refs: pack_kernel(*refs, tiles=tiles, depths=depths),
        out_shape=[
            jax.ShapeDtypeStruct((tiles, depths, 5, 1, lanes), jnp.float32),
            jax.ShapeDtypeStruct((2 * EDGE, lanes), jnp.float32),
        ],
        in_specs=[pl.BlockSpec(memory_space=pltpu.SMEM)] + [pl.BlockSpec(memory_space=pltpu.HBM)] * 2,
        out_specs=[vmem, vmem],
        scratch_shapes=[
            pltpu.VMEM((slots, columns, rows), jnp.float32),
            pltpu.VMEM((columns, rows), jnp.int32),
            pltpu.SemaphoreType.DMA((2,)),
        ],
        compiler_params=params,
        name="pack",
    )(view_flip, *(pltpu.with_memory_space_constraint(x, pltpu.HBM) for x in inputs))
    sent = outgoing.reshape(zblocks, 5, 1, lanes)
    arrived = lax.all_to_all(sent, ("tile", "depth"), split_axis=0, concat_axis=0, tiled=True)
    return pl.pallas_call(
        lambda *refs: render_kernel(*refs, strip=strip, band=band, samples=EDGE * zblocks),
        out_shape=jax.ShapeDtypeStruct((4, strip * EDGE, band * EDGE), jnp.float32),
        in_specs=[vmem, vmem],
        out_specs=vmem,
        scratch_shapes=[pltpu.VMEM((slots, zblocks, lanes), jnp.float32)],
        compiler_params=params,
        name="render",
    )(sign, arrived.reshape(outgoing.shape))


def solution(mesh):
    placed = (P(None, "depth", "tile", None, None), P("depth", "tile", None, None), P("tile"))
    return jax.shard_map(
        per_device, mesh=mesh, in_specs=placed, out_specs=P(None, "tile", "depth"), check_vma=False
    )
```

profile of v0, /device:TPU:0, one launch (start us, length us, event | category | flops | bytes accessed | tf_op | source)
XLA Modules:
  0.0 18.7 jit_solution(4320406052616574655)
XLA Ops:
  0.7 1.2 %pack.1 = (f32[8,4,5,1,128]{4,3,2,1,0:T(1,128)S(1)}, f32[8,128]{1,0:T(8,128)S(1)}) custom-call(s32[1]{0:T(128)S(6)} %copy.4.refs_0_, f32[8,32,128]{2,1,0:T(8,128)} %bitcast.6, s32[32,128]{1,0:T(8,128)} %bitcast.7), custom_call_target="tpu_custom_call" | custom-call | tf_op jit(solution)/shard_map/pack/pallas_call | solution.py:181
  1.8 14.8 %all_to_all.5 = f32[32,5,1,128]{3,2,1,0:T(1,128)S(1)} all-to-all(f32[32,5,1,128]{3,2,1,0:T(1,128)S(1)} %bitcast.5), channel_id=1, replica_groups=mesh['tile'=8,'depth'=4] {'tile','depth'}, dimensions={0} | all-to-all | bytes 163840 | tf_op jit(solution)/shard_map/all_to_all | solution.py:198
  16.6 2.1 %render.1 = f32[4,16,128]{2,1,0:T(8,128)} custom-call(f32[8,128]{1,0:T(8,128)S(1)} %get-tuple-element.7.refs_0_, f32[8,4,5,1,128]{4,3,2,1,0:T(1,128)S(1)} %bitcast.4), custom_call_target="tpu_custom_call" | custom-call | tf_op jit(solution)/shard_map/render/pallas_call | solution.py:199
where the time goes:
time: 18.9 us; the launch traced here: 18.7 us
  blocking collectives  14.8 us (78%)
  Pallas kernels  3.24 us (17%)
  between operations  0.66 us (3%)
    all_to_all x1, blocking collectives, per_device(): lax.all_to_all(sent, ('tile', 'depth'), split_axis=0, concat_axis=0, tile...  14.8 us
    pallas_call x1, Pallas kernels, per_device(): pl.pallas_call(lambda *refs: render_kernel(*refs, strip=strip, band=band,...  2.07 us
    pallas_call x1, Pallas kernels, per_device(): pl.pallas_call(lambda *refs: pack_kernel(*refs, tiles=tiles, depths=depth...  1.17 us

commit v1 on v0

--- a/solution.py
+++ b/solution.py
@@ -24,7 +24,7 @@
 
 
 def pack_kernel(
-    flip_ref, coef_hbm, keep_hbm, out_ref, sign_ref, coef_ref, keep_ref, arrival, *, tiles, depths
+    flip_ref, coef_hbm, keep_hbm, out_ref, sign_ref, coef_ref, keep_ref, rows_ref, arrival, *, tiles, depths
 ):
     _, columns, rows = coef_ref.shape
     strip = columns // tiles
@@ -63,11 +63,16 @@
             merged = gathered[0]
             for b in range(1, strip):
                 merged = jnp.where(column == b, gathered[b], merged)
-            out_ref[:, d, q, 0, :] = merged[:, : 2 * half]
+            rows_ref[d, q] = merged[:, : 2 * half]
+
+
+    for d in range(depths):
+        for t in range(tiles):
+            out_ref[depths - 1 - d, tiles - 1 - t, :, 0, :] = rows_ref[d, :, t, :]
 
 
 def unpack(packed_ref, coef_ref):
-    tiles, depths, _, _, lanes = packed_ref.shape
+    depths, tiles, _, _, lanes = packed_ref.shape
     zblocks = tiles * depths
     first = lax.broadcasted_iota(jnp.int32, (zblocks, lanes), 1) < lanes // 2
     row = [packed_ref[:, :, q, 0, :].reshape(zblocks, lanes) for q in range(5)]
@@ -83,7 +88,6 @@
 def render_kernel(sign_ref, packed_ref, out_ref, coef_ref, *, strip, band, samples):
     unpack(packed_ref, coef_ref)
     slots, zblocks, lanes = coef_ref.shape
-    tiles, depths = packed_ref.shape[:2]
     sign = sign_ref[...]
     flipped = jnp.max(sign) < 0.0
     b1 = [cosine(1, i) for i in range(EDGE)]
@@ -115,7 +119,7 @@
 
     def block(step, state):
         source = jnp.where(flipped, zblocks - 1 - step, step)
-        zb = source % tiles * depths + source // tiles
+        zb = zblocks - 1 - source
         a = [
             jnp.broadcast_to(coef_ref[k, pl.ds(zb, 1), :], (2 * EDGE, lanes)) for k in range(slots)
         ]
@@ -145,7 +149,7 @@
     zero = jnp.zeros((2 * EDGE, lanes), jnp.float32)
     one = jnp.ones((2 * EDGE, lanes), jnp.float32)
     start = (zero, one, zero, zero, zero)
-    state = lax.fori_loop(0, zblocks, block, (start, start), unroll=4)
+    state = lax.fori_loop(0, zblocks, block, (start, start), unroll=8)
 
     width = band * EDGE
     pick = lax.broadcasted_iota(jnp.int32, (2 * EDGE, width), 1)
@@ -181,7 +185,7 @@
     outgoing, sign = pl.pallas_call(
         lambda *refs: pack_kernel(*refs, tiles=tiles, depths=depths),
         out_shape=[
-            jax.ShapeDtypeStruct((tiles, depths, 5, 1, lanes), jnp.float32),
+            jax.ShapeDtypeStruct((depths, tiles, 5, 1, lanes), jnp.float32),
             jax.ShapeDtypeStruct((2 * EDGE, lanes), jnp.float32),
         ],
         in_specs=[pl.BlockSpec(memory_space=pltpu.SMEM)] + [pl.BlockSpec(memory_space=pltpu.HBM)] * 2,
@@ -189,13 +193,17 @@
         scratch_shapes=[
             pltpu.VMEM((slots, columns, rows), jnp.float32),
             pltpu.VMEM((columns, rows), jnp.int32),
+            pltpu.VMEM((depths, 5, tiles, lanes), jnp.float32),
             pltpu.SemaphoreType.DMA((2,)),
         ],
         compiler_params=params,
         name="pack",
     )(view_flip, *(pltpu.with_memory_space_constraint(x, pltpu.HBM) for x in inputs))
     sent = outgoing.reshape(zblocks, 5, 1, lanes)
-    arrived = lax.all_to_all(sent, ("tile", "depth"), split_axis=0, concat_axis=0, tiled=True)
+    falling = [list(range(zblocks - 1, -1, -1))]
+    arrived = lax.all_to_all(
+        sent, ("depth", "tile"), split_axis=0, concat_axis=0, tiled=True, axis_index_groups=falling
+    )
     return pl.pallas_call(
         lambda *refs: render_kernel(*refs, strip=strip, band=band, samples=EDGE * zblocks),
         out_shape=jax.ShapeDtypeStruct((4, strip * EDGE, band * EDGE), jnp.float32),

time: 18.9 us -> 18.5 us (0.979)
  blocking collectives: 14.8 us -> 14.6 us
    all_to_all x1, blocking collectives: 14.8 us -> 14.6 us  [per_device(): lax.all_to_all(sent, ('depth', 'tile'), split_axis=0, concat_axis=0, tile...]
where the time goes in v1:
time: 18.5 us; the launch traced here: 18.4 us
  blocking collectives  14.6 us (79%)
  Pallas kernels  3.1 us (17%)
  between operations  0.66 us (4%)
    all_to_all x1, blocking collectives, per_device(): lax.all_to_all(sent, ('depth', 'tile'), split_axis=0, concat_axis=0, tile...  14.6 us
    pallas_call x1, Pallas kernels, per_device(): pl.pallas_call(lambda *refs: render_kernel(*refs, strip=strip, band=band,...  1.91 us
    pallas_call x1, Pallas kernels, per_device(): pl.pallas_call(lambda *refs: pack_kernel(*refs, tiles=tiles, depths=depth...  1.19 us

profile of v1, /device:TPU:0, one launch (start us, length us, event | category | flops | bytes accessed | tf_op | source)
XLA Modules:
  0.0 18.4 jit_solution(5753732669880652995)
XLA Ops:
  0.7 1.2 %pack.1 = (f32[4,8,5,1,128]{4,3,2,1,0:T(1,128)S(1)}, f32[8,128]{1,0:T(8,128)S(1)}) custom-call(s32[1]{0:T(128)S(6)} %copy.4.refs_0_, f32[8,32,128]{2,1,0:T(8,128)} %bitcast.6, s32[32,128]{1,0:T(8,128)} %bitcast.7), custom_call_target="tpu_custom_call" | custom-call | tf_op jit(solution)/shard_map/pack/pallas_call | solution.py:185
  1.9 14.6 %all_to_all.5 = f32[32,5,1,128]{3,2,1,0:T(1,128)S(1)} all-to-all(f32[32,5,1,128]{3,2,1,0:T(1,128)S(1)} %bitcast.5), channel_id=1, replica_groups={{31,27,23,19,15,11,7,3,30,26,22,18,14,10,6,2,29,25,21,17,13,9,5,1,28,24..., dimensions={0} | all-to-all | bytes 163840 | tf_op jit(solution)/shard_map/all_to_all | solution.py:204
  16.5 1.9 %render.1 = f32[4,16,128]{2,1,0:T(8,128)} custom-call(f32[8,128]{1,0:T(8,128)S(1)} %get-tuple-element.7.refs_0_, f32[4,8,5,1,128]{4,3,2,1,0:T(1,128)S(1)} %bitcast.4), custom_call_target="tpu_custom_call" | custom-call | tf_op jit(solution)/shard_map/render/pallas_call | solution.py:207

commit v2 on v1

--- a/solution.py
+++ b/solution.py
@@ -29,7 +29,7 @@
     _, columns, rows = coef_ref.shape
     strip = columns // tiles
     band = rows // depths
-    moves = ((coef_hbm, coef_ref), (keep_hbm, keep_ref))
+    moves = [(keep_hbm, keep_ref)] + [(coef_hbm.at[k], coef_ref.at[k]) for k in range(8)]
     fetches = [pltpu.make_async_copy(a, b, arrival.at[i]) for i, (a, b) in enumerate(moves)]
     for fetch in fetches:
         fetch.start()
@@ -114,7 +114,8 @@
     c_z = jnp.full((2 * EDGE, lanes), 0.25 * LOG2E * b1[0], jnp.float32) * sign
     c_zy = (0.5 * LOG2E * b1[0]) * y1 * sign
     ratio = b1[1] / b1[0]
-    blue_factor = math.exp(-1.5)
+    blue_one = 2.0**-20
+    blue_factor = blue_one * math.exp(-1.5)
     fade = -1.5 / samples
 
     def block(step, state):
@@ -140,16 +141,18 @@
                 after = jnp.exp2(fade * depth)
                 weight = before - after
                 before = after
-                red = red + weight / one_u
+                blue_u = blue_one + blue_factor * v
+                shared = weight / (one_u * blue_u)
+                red = red + shared * blue_u
                 green = green + weight * jnp.exp2(f * (f * (-1.0 / LOG2E)))
-                blue = blue + weight / (1.0 + blue_factor * v)
+                blue = blue + shared * one_u
             halves.append((depth, before, red, green, blue))
         return tuple(halves)
 
     zero = jnp.zeros((2 * EDGE, lanes), jnp.float32)
     one = jnp.ones((2 * EDGE, lanes), jnp.float32)
     start = (zero, one, zero, zero, zero)
-    state = lax.fori_loop(0, zblocks, block, (start, start), unroll=8)
+    state = lax.fori_loop(0, zblocks, block, (start, start), unroll=16)
 
     width = band * EDGE
     pick = lax.broadcasted_iota(jnp.int32, (2 * EDGE, width), 1)
@@ -159,7 +162,7 @@
     outs = []
     for _, before, red, green, blue in state:
         opacity = 1.0 - before
-        outs.append((opacity - red, green, blue, opacity))
+        outs.append((opacity - red, green, blue * blue_one, opacity))
     for ch in range(4):
         for b in range(strip):
             index = place + b * (band // 2)
@@ -194,7 +197,7 @@
             pltpu.VMEM((slots, columns, rows), jnp.float32),
             pltpu.VMEM((columns, rows), jnp.int32),
             pltpu.VMEM((depths, 5, tiles, lanes), jnp.float32),
-            pltpu.SemaphoreType.DMA((2,)),
+            pltpu.SemaphoreType.DMA((1 + slots,)),
         ],
         compiler_params=params,
         name="pack",

time: 18.5 us -> 18.7 us (1.011); the launches traced: 18.4 us -> 18.3 us
  no operation moved by 1% of the time
where the time goes in v2:
time: 18.7 us; the launch traced here: 18.3 us
  blocking collectives  14.6 us (78%)
  Pallas kernels  3.06 us (16%)
  between operations  0.66 us (4%)
    all_to_all x1, blocking collectives, per_device(): lax.all_to_all(sent, ('depth', 'tile'), split_axis=0, concat_axis=0, tile...  14.6 us
    pallas_call x1, Pallas kernels, per_device(): pl.pallas_call(lambda *refs: render_kernel(*refs, strip=strip, band=band,...  1.85 us
    pallas_call x1, Pallas kernels, per_device(): pl.pallas_call(lambda *refs: pack_kernel(*refs, tiles=tiles, depths=depth...  1.2 us

profile of v2, /device:TPU:0, one launch (start us, length us, event | category | flops | bytes accessed | tf_op | source)
XLA Modules:
  0.0 18.3 jit_solution(17284148075077946784)
XLA Ops:
  0.7 1.2 %pack.1 = (f32[4,8,5,1,128]{4,3,2,1,0:T(1,128)S(1)}, f32[8,128]{1,0:T(8,128)S(1)}) custom-call(s32[1]{0:T(128)S(6)} %copy.4.refs_0_, f32[8,32,128]{2,1,0:T(8,128)} %bitcast.6, s32[32,128]{1,0:T(8,128)} %bitcast.7), custom_call_target="tpu_custom_call" | custom-call | tf_op jit(solution)/shard_map/pack/pallas_call | solution.py:188
  1.9 14.6 %all_to_all.5 = f32[32,5,1,128]{3,2,1,0:T(1,128)S(1)} all-to-all(f32[32,5,1,128]{3,2,1,0:T(1,128)S(1)} %bitcast.5), channel_id=1, replica_groups={{31,27,23,19,15,11,7,3,30,26,22,18,14,10,6,2,29,25,21,17,13,9,5,1,28,24..., dimensions={0} | all-to-all | bytes 163840 | tf_op jit(solution)/shard_map/all_to_all | solution.py:207
  16.5 1.9 %render.1 = f32[4,16,128]{2,1,0:T(8,128)} custom-call(f32[8,128]{1,0:T(8,128)S(1)} %get-tuple-element.7.refs_0_, f32[4,8,5,1,128]{4,3,2,1,0:T(1,128)S(1)} %bitcast.4), custom_call_target="tpu_custom_call" | custom-call | tf_op jit(solution)/shard_map/render/pallas_call | solution.py:210

commit v3 on v2

--- a/solution.py
+++ b/solution.py
@@ -122,7 +122,7 @@
         source = jnp.where(flipped, zblocks - 1 - step, step)
         zb = zblocks - 1 - source
         a = [
-            jnp.broadcast_to(coef_ref[k, pl.ds(zb, 1), :], (2 * EDGE, lanes)) for k in range(slots)
+            coef_ref[k, pl.ds(zb, 2 * EDGE, stride=0), :] for k in range(slots)
         ]
         even = a[0] * c_dc + a[2] * c_x1 + a[4] * c_y2 + a[6] * c_x2
         odd = a[1] * c_y1 + a[5] * c_xy

time: 18.7 us -> 18.7 us (level)
  no operation moved by 1% of the time
where the time goes in v3:
time: 18.7 us; the launch traced here: 18.3 us
  blocking collectives  14.6 us (78%)
  Pallas kernels  3.07 us (16%)
  between operations  0.66 us (4%)
    all_to_all x1, blocking collectives, per_device(): lax.all_to_all(sent, ('depth', 'tile'), split_axis=0, concat_axis=0, tile...  14.6 us
    pallas_call x1, Pallas kernels, per_device(): pl.pallas_call(lambda *refs: render_kernel(*refs, strip=strip, band=band,...  1.86 us
    pallas_call x1, Pallas kernels, per_device(): pl.pallas_call(lambda *refs: pack_kernel(*refs, tiles=tiles, depths=depth...  1.2 us

profile of v3, /device:TPU:0, one launch (start us, length us, event | category | flops | bytes accessed | tf_op | source)
XLA Modules:
  0.0 18.3 jit_solution(18005937153776983100)
XLA Ops:
  0.7 1.2 %pack.1 = (f32[4,8,5,1,128]{4,3,2,1,0:T(1,128)S(1)}, f32[8,128]{1,0:T(8,128)S(1)}) custom-call(s32[1]{0:T(128)S(6)} %copy.4.refs_0_, f32[8,32,128]{2,1,0:T(8,128)} %bitcast.6, s32[32,128]{1,0:T(8,128)} %bitcast.7), custom_call_target="tpu_custom_call" | custom-call | tf_op jit(solution)/shard_map/pack/pallas_call | solution.py:188
  1.9 14.6 %all_to_all.5 = f32[32,5,1,128]{3,2,1,0:T(1,128)S(1)} all-to-all(f32[32,5,1,128]{3,2,1,0:T(1,128)S(1)} %bitcast.5), channel_id=1, replica_groups={{31,27,23,19,15,11,7,3,30,26,22,18,14,10,6,2,29,25,21,17,13,9,5,1,28,24..., dimensions={0} | all-to-all | bytes 163840 | tf_op jit(solution)/shard_map/all_to_all | solution.py:207
  16.5 1.9 %render.1 = f32[4,16,128]{2,1,0:T(8,128)} custom-call(f32[8,128]{1,0:T(8,128)S(1)} %get-tuple-element.7.refs_0_, f32[4,8,5,1,128]{4,3,2,1,0:T(1,128)S(1)} %bitcast.4), custom_call_target="tpu_custom_call" | custom-call | tf_op jit(solution)/shard_map/render/pallas_call | solution.py:210

commit v4 on v2

--- a/solution.py
+++ b/solution.py
@@ -24,17 +24,17 @@
 
 
 def pack_kernel(
-    flip_ref, coef_hbm, keep_hbm, out_ref, sign_ref, coef_ref, keep_ref, rows_ref, arrival, *, tiles, depths
+    flip_ref, coef_hbm, keep_hbm, out_ref, sign_ref, coef_ref, keep_ref, arrival, *, tiles, depths
 ):
     _, columns, rows = coef_ref.shape
     strip = columns // tiles
     band = rows // depths
-    moves = [(keep_hbm, keep_ref)] + [(coef_hbm.at[k], coef_ref.at[k]) for k in range(8)]
-    fetches = [pltpu.make_async_copy(a, b, arrival.at[i]) for i, (a, b) in enumerate(moves)]
-    for fetch in fetches:
-        fetch.start()
-    for fetch in fetches:
-        fetch.wait()
+    fetch_keep = pltpu.make_async_copy(keep_hbm, keep_ref, arrival.at[8])
+    fetches = [pltpu.make_async_copy(coef_hbm.at[k], coef_ref.at[k], arrival.at[k]) for k in range(8)]
+    fetch_keep.start()
+    for k in (1, 7, 2, 6, 3, 5, 4, 0):
+        fetches[k].start()
+    fetch_keep.wait()
     lane = lax.broadcasted_iota(jnp.int32, (tiles, rows), 1)
     even = lane % 2 == 0
 
@@ -42,40 +42,35 @@
         return jnp.take_along_axis(values, index, axis=1)
 
     other = lane + 1 - 2 * (lane % 2)
-    packed = []
-    for b in range(strip):
-        mine = pl.ds(b, tiles, stride=strip)
-        keep = keep_ref[mine, :]
-        slot = [coef_ref[k, mine, :] for k in range(8)]
-        result = [slot[0]]
-        for q in (1, 2, 3, 4):
-            result.append(jnp.where(keep > q, slot[q], take(slot[8 - q], other)))
-        result[4] = jnp.where(even, result[4], (9 - keep).astype(jnp.float32))
-        packed.append(result)
     sign_ref[...] = jnp.full(sign_ref.shape, 1 - 2 * flip_ref[0], jnp.int32).astype(jnp.float32)
     half = strip * band // 2
     parity = lane // half % 2
     column = lane // (band // 2) % strip
     source = lane % (band // 2) * 2 + parity
-    for d in range(depths):
-        for q in range(5):
-            gathered = [take(packed[b][q], source + d * band) for b in range(strip)]
+    mine = [pl.ds(b, tiles, stride=strip) for b in range(strip)]
+    keep = [keep_ref[rows_b, :] for rows_b in mine]
+    for q in (1, 2, 3, 4, 0):
+        for k in (q, 8 - q) if q % 4 else (q,):
+            fetches[k].wait()
+        packed = [coef_ref[q, rows_b, :] for rows_b in mine]
+        if q > 0:
+            turned = [take(coef_ref[8 - q, rows_b, :], other) for rows_b in mine]
+            packed = [jnp.where(keep[b] > q, packed[b], turned[b]) for b in range(strip)]
+        if q == 4:
+            packed = [jnp.where(even, packed[b], (9 - keep[b]).astype(jnp.float32)) for b in range(strip)]
+        for d in range(depths):
+            gathered = [take(packed[b], source + d * band) for b in range(strip)]
             merged = gathered[0]
             for b in range(1, strip):
                 merged = jnp.where(column == b, gathered[b], merged)
-            rows_ref[d, q] = merged[:, : 2 * half]
-
-
-    for d in range(depths):
-        for t in range(tiles):
-            out_ref[depths - 1 - d, tiles - 1 - t, :, 0, :] = rows_ref[d, :, t, :]
+            start = (depths - 1 - d) * tiles * 5 + q
+            out_ref[pl.ds(start, tiles, stride=5), :] = merged[:, : 2 * half]
 
 
 def unpack(packed_ref, coef_ref):
-    depths, tiles, _, _, lanes = packed_ref.shape
-    zblocks = tiles * depths
+    zblocks, lanes = packed_ref.shape[0] // 5, packed_ref.shape[1]
     first = lax.broadcasted_iota(jnp.int32, (zblocks, lanes), 1) < lanes // 2
-    row = [packed_ref[:, :, q, 0, :].reshape(zblocks, lanes) for q in range(5)]
+    row = [packed_ref[pl.ds(q, zblocks, stride=5), :] for q in range(5)]
     turned = [None] + [swap_halves(row[q]) for q in (1, 2, 3, 4)]
     keep = jnp.where(first, turned[4], 9.0 - row[4])
     slot = [row[0]] + [jnp.where(keep > q, row[q], 0.0) for q in (1, 2, 3)]
@@ -85,7 +80,7 @@
         coef_ref[k] = slot[k]
 
 
-def render_kernel(sign_ref, packed_ref, out_ref, coef_ref, *, strip, band, samples):
+def render_kernel(sign_ref, packed_ref, out_ref, coef_ref, *, strip, band, samples, tiles, depths):
     unpack(packed_ref, coef_ref)
     slots, zblocks, lanes = coef_ref.shape
     sign = sign_ref[...]
@@ -120,7 +115,7 @@
 
     def block(step, state):
         source = jnp.where(flipped, zblocks - 1 - step, step)
-        zb = zblocks - 1 - source
+        zb = (depths - 1 - source // tiles) * tiles + source % tiles
         a = [
             jnp.broadcast_to(coef_ref[k, pl.ds(zb, 1), :], (2 * EDGE, lanes)) for k in range(slots)
         ]
@@ -188,7 +183,7 @@
     outgoing, sign = pl.pallas_call(
         lambda *refs: pack_kernel(*refs, tiles=tiles, depths=depths),
         out_shape=[
-            jax.ShapeDtypeStruct((depths, tiles, 5, 1, lanes), jnp.float32),
+            jax.ShapeDtypeStruct((zblocks * 5, lanes), jnp.float32),
             jax.ShapeDtypeStruct((2 * EDGE, lanes), jnp.float32),
         ],
         in_specs=[pl.BlockSpec(memory_space=pltpu.SMEM)] + [pl.BlockSpec(memory_space=pltpu.HBM)] * 2,
@@ -196,19 +191,20 @@
         scratch_shapes=[
             pltpu.VMEM((slots, columns, rows), jnp.float32),
             pltpu.VMEM((columns, rows), jnp.int32),
-            pltpu.VMEM((depths, 5, tiles, lanes), jnp.float32),
             pltpu.SemaphoreType.DMA((1 + slots,)),
         ],
         compiler_params=params,
         name="pack",
     )(view_flip, *(pltpu.with_memory_space_constraint(x, pltpu.HBM) for x in inputs))
     sent = outgoing.reshape(zblocks, 5, 1, lanes)
-    falling = [list(range(zblocks - 1, -1, -1))]
+    falling = [[d * tiles + t for d in reversed(range(depths)) for t in range(tiles)]]
     arrived = lax.all_to_all(
         sent, ("depth", "tile"), split_axis=0, concat_axis=0, tiled=True, axis_index_groups=falling
     )
     return pl.pallas_call(
-        lambda *refs: render_kernel(*refs, strip=strip, band=band, samples=EDGE * zblocks),
+        lambda *refs: render_kernel(
+            *refs, strip=strip, band=band, samples=EDGE * zblocks, tiles=tiles, depths=depths
+        ),
         out_shape=jax.ShapeDtypeStruct((4, strip * EDGE, band * EDGE), jnp.float32),
         in_specs=[vmem, vmem],
         out_specs=vmem,

time: 18.7 us -> 19.3 us (1.032)
  Pallas kernels: 3.06 us -> 3.52 us
  blocking collectives: 14.6 us -> 14.8 us
    pallas_call x1, Pallas kernels: 1.2 us -> 1.65 us  [per_device(): pl.pallas_call(lambda *refs: pack_kernel(*refs, tiles=tiles, depths=depth...]
    all_to_all x1, blocking collectives: 14.6 us -> 14.8 us  [per_device(): lax.all_to_all(sent, ('depth', 'tile'), split_axis=0, concat_axis=0, tile...]
where the time goes in v4:
time: 19.3 us; the launch traced here: 19 us
  blocking collectives  14.8 us (77%)
  Pallas kernels  3.52 us (18%)
  between operations  0.66 us (3%)
    all_to_all x1, blocking collectives, per_device(): lax.all_to_all(sent, ('depth', 'tile'), split_axis=0, concat_axis=0, tile...  14.8 us
    pallas_call x1, Pallas kernels, per_device(): pl.pallas_call(lambda *refs: render_kernel(*refs, strip=strip, band=band,...  1.86 us
    pallas_call x1, Pallas kernels, per_device(): pl.pallas_call(lambda *refs: pack_kernel(*refs, tiles=tiles, depths=depth...  1.65 us

profile of v4, /device:TPU:0, one launch (start us, length us, event | category | flops | bytes accessed | tf_op | source)
XLA Modules:
  0.0 19.0 jit_solution(14486535729762454570)
XLA Ops:
  0.7 1.7 %pack.1 = (f32[160,128]{1,0:T(8,128)S(1)}, f32[8,128]{1,0:T(8,128)S(1)}) custom-call(s32[1]{0:T(128)S(6)} %copy.5.refs_0_, f32[8,32,128]{2,1,0:T(8,128)} %bitcast.6, s32[32,128]{1,0:T(8,128)} %bitcast.7), custom_call_target="tpu_custom_call" | custom-call | tf_op jit(solution)/shard_map/pack/pallas_call | solution.py:183
  2.3 14.8 %all_to_all.5 = f32[32,5,1,128]{3,2,1,0:T(1,128)S(1)} all-to-all(f32[32,5,1,128]{3,2,1,0:T(1,128)S(1)} %bitcast.5), channel_id=1, replica_groups={{3,7,11,15,19,23,27,31,2,6,10,14,18,22,26,30,1,5,9,13,17,21,25,29,0,4,8..., dimensions={0} | all-to-all | bytes 163840 | tf_op jit(solution)/shard_map/all_to_all | solution.py:201
  17.2 1.9 %render.1 = f32[4,16,128]{2,1,0:T(8,128)} custom-call(f32[8,128]{1,0:T(8,128)S(1)} %get-tuple-element.7.refs_0_, f32[160,128]{1,0:T(8,128)S(1)} %bitcast.4), custom_call_target="tpu_custom_call" | custom-call | tf_op jit(solution)/shard_map/render/pallas_call | solution.py:204

commit v5 on v4

--- a/solution.py
+++ b/solution.py
@@ -23,18 +23,23 @@
     return jnp.concatenate([values[:, half:], values[:, :half]], axis=1)
 
 
+def listed_at(t, d, tiles, depths):
+    return (tiles - 1 - t) * depths + depths - 1 - d
+
+
 def pack_kernel(
-    flip_ref, coef_hbm, keep_hbm, out_ref, sign_ref, coef_ref, keep_ref, arrival, *, tiles, depths
+    flip_ref, coef_hbm, keep_hbm, out_ref, sign_ref, coef_ref, keep_ref, rows_ref, arrival, *, tiles, depths
 ):
     _, columns, rows = coef_ref.shape
     strip = columns // tiles
     band = rows // depths
     fetch_keep = pltpu.make_async_copy(keep_hbm, keep_ref, arrival.at[8])
     fetches = [pltpu.make_async_copy(coef_hbm.at[k], coef_ref.at[k], arrival.at[k]) for k in range(8)]
-    fetch_keep.start()
-    for k in (1, 7, 2, 6, 3, 5, 4, 0):
-        fetches[k].start()
-    fetch_keep.wait()
+    fetches.append(fetch_keep)
+    for fetch in fetches:
+        fetch.start()
+    for fetch in fetches:
+        fetch.wait()
     lane = lax.broadcasted_iota(jnp.int32, (tiles, rows), 1)
     even = lane % 2 == 0
 
@@ -50,8 +55,6 @@
     mine = [pl.ds(b, tiles, stride=strip) for b in range(strip)]
     keep = [keep_ref[rows_b, :] for rows_b in mine]
     for q in (1, 2, 3, 4, 0):
-        for k in (q, 8 - q) if q % 4 else (q,):
-            fetches[k].wait()
         packed = [coef_ref[q, rows_b, :] for rows_b in mine]
         if q > 0:
             turned = [take(coef_ref[8 - q, rows_b, :], other) for rows_b in mine]
@@ -63,8 +66,10 @@
             merged = gathered[0]
             for b in range(1, strip):
                 merged = jnp.where(column == b, gathered[b], merged)
-            start = (depths - 1 - d) * tiles * 5 + q
-            out_ref[pl.ds(start, tiles, stride=5), :] = merged[:, : 2 * half]
+            rows_ref[d, q] = merged[:, : 2 * half]
+    for d in range(depths):
+        for t in range(tiles):
+            out_ref[pl.ds(listed_at(t, d, tiles, depths) * 5, 5), :] = rows_ref[d, :, t, :]
 
 
 def unpack(packed_ref, coef_ref):
@@ -115,7 +120,7 @@
 
     def block(step, state):
         source = jnp.where(flipped, zblocks - 1 - step, step)
-        zb = (depths - 1 - source // tiles) * tiles + source % tiles
+        zb = listed_at(source % tiles, source // tiles, tiles, depths)
         a = [
             jnp.broadcast_to(coef_ref[k, pl.ds(zb, 1), :], (2 * EDGE, lanes)) for k in range(slots)
         ]
@@ -191,15 +196,17 @@
         scratch_shapes=[
             pltpu.VMEM((slots, columns, rows), jnp.float32),
             pltpu.VMEM((columns, rows), jnp.int32),
+            pltpu.VMEM((depths, 5, tiles, lanes), jnp.float32),
             pltpu.SemaphoreType.DMA((1 + slots,)),
         ],
         compiler_params=params,
         name="pack",
     )(view_flip, *(pltpu.with_memory_space_constraint(x, pltpu.HBM) for x in inputs))
     sent = outgoing.reshape(zblocks, 5, 1, lanes)
-    falling = [[d * tiles + t for d in reversed(range(depths)) for t in range(tiles)]]
+    devices = [(t, d) for d in range(depths) for t in range(tiles)]
+    listed = sorted(range(zblocks), key=lambda i: listed_at(*devices[i], tiles, depths))
     arrived = lax.all_to_all(
-        sent, ("depth", "tile"), split_axis=0, concat_axis=0, tiled=True, axis_index_groups=falling
+        sent, ("depth", "tile"), split_axis=0, concat_axis=0, tiled=True, axis_index_groups=[listed]
     )
     return pl.pallas_call(
         lambda *refs: render_kernel(

time: 19.3 us -> 18.7 us (0.969)
  Pallas kernels: 3.52 us -> 3.2 us
  blocking collectives: 14.8 us -> 14.5 us
    all_to_all x1, blocking collectives: 14.8 us -> 14.5 us  [per_device(): lax.all_to_all(sent, ('depth', 'tile'), split_axis=0, concat_axis=0, tile...]
    pallas_call x1, Pallas kernels: 1.65 us -> 1.33 us  [per_device(): pl.pallas_call(lambda *refs: pack_kernel(*refs, tiles=tiles, depths=depth...]
where the time goes in v5:
time: 18.7 us; the launch traced here: 18.4 us
  blocking collectives  14.5 us (78%)
  Pallas kernels  3.2 us (17%)
  between operations  0.66 us (4%)
    all_to_all x1, blocking collectives, per_device(): lax.all_to_all(sent, ('depth', 'tile'), split_axis=0, concat_axis=0, tile...  14.5 us
    pallas_call x1, Pallas kernels, per_device(): pl.pallas_call(lambda *refs: render_kernel(*refs, strip=strip, band=band,...  1.86 us
    pallas_call x1, Pallas kernels, per_device(): pl.pallas_call(lambda *refs: pack_kernel(*refs, tiles=tiles, depths=depth...  1.33 us

profile of v5, /device:TPU:0, one launch (start us, length us, event | category | flops | bytes accessed | tf_op | source)
XLA Modules:
  0.0 18.4 jit_solution(14988047642786357613)
XLA Ops:
  0.7 1.3 %pack.1 = (f32[160,128]{1,0:T(8,128)S(1)}, f32[8,128]{1,0:T(8,128)S(1)}) custom-call(s32[1]{0:T(128)S(6)} %copy.5.refs_0_, f32[8,32,128]{2,1,0:T(8,128)} %bitcast.6, s32[32,128]{1,0:T(8,128)} %bitcast.7), custom_call_target="tpu_custom_call" | custom-call | tf_op jit(solution)/shard_map/pack/pallas_call | solution.py:188
  2.0 14.5 %all_to_all.5 = f32[32,5,1,128]{3,2,1,0:T(1,128)S(1)} all-to-all(f32[32,5,1,128]{3,2,1,0:T(1,128)S(1)} %bitcast.5), channel_id=1, replica_groups={{31,30,29,28,27,26,25,24,23,22,21,20,19,18,17,16,15,14,13,12,11,10,9,8,..., dimensions={0} | all-to-all | bytes 163840 | tf_op jit(solution)/shard_map/all_to_all | solution.py:208
  16.5 1.9 %render.1 = f32[4,16,128]{2,1,0:T(8,128)} custom-call(f32[8,128]{1,0:T(8,128)S(1)} %get-tuple-element.7.refs_0_, f32[160,128]{1,0:T(8,128)S(1)} %bitcast.4), custom_call_target="tpu_custom_call" | custom-call | tf_op jit(solution)/shard_map/render/pallas_call | solution.py:211

commit v6 on v2

--- a/solution.py
+++ b/solution.py
@@ -23,13 +23,23 @@
     return jnp.concatenate([values[:, half:], values[:, :half]], axis=1)
 
 
+def listed_at(t, d, tiles, depths):
+    turned, size = 0, 1
+    while 2 * size <= depths:
+        turned = turned + d // size % 2 * (depths // (2 * size))
+        size *= 2
+    if size != depths:
+        turned = d
+    return tiles * depths - 1 - turned * tiles - t
+
+
 def pack_kernel(
     flip_ref, coef_hbm, keep_hbm, out_ref, sign_ref, coef_ref, keep_ref, rows_ref, arrival, *, tiles, depths
 ):
     _, columns, rows = coef_ref.shape
     strip = columns // tiles
     band = rows // depths
-    moves = [(keep_hbm, keep_ref)] + [(coef_hbm.at[k], coef_ref.at[k]) for k in range(8)]
+    moves = ((coef_hbm, coef_ref), (keep_hbm, keep_ref))
     fetches = [pltpu.make_async_copy(a, b, arrival.at[i]) for i, (a, b) in enumerate(moves)]
     for fetch in fetches:
         fetch.start()
@@ -68,14 +78,13 @@
 
     for d in range(depths):
         for t in range(tiles):
-            out_ref[depths - 1 - d, tiles - 1 - t, :, 0, :] = rows_ref[d, :, t, :]
+            out_ref[listed_at(t, d, tiles, depths), :, 0, :] = rows_ref[d, :, t, :]
 
 
 def unpack(packed_ref, coef_ref):
-    depths, tiles, _, _, lanes = packed_ref.shape
-    zblocks = tiles * depths
+    zblocks, _, _, lanes = packed_ref.shape
     first = lax.broadcasted_iota(jnp.int32, (zblocks, lanes), 1) < lanes // 2
-    row = [packed_ref[:, :, q, 0, :].reshape(zblocks, lanes) for q in range(5)]
+    row = [packed_ref[:, q, 0, :] for q in range(5)]
     turned = [None] + [swap_halves(row[q]) for q in (1, 2, 3, 4)]
     keep = jnp.where(first, turned[4], 9.0 - row[4])
     slot = [row[0]] + [jnp.where(keep > q, row[q], 0.0) for q in (1, 2, 3)]
@@ -85,7 +94,7 @@
         coef_ref[k] = slot[k]
 
 
-def render_kernel(sign_ref, packed_ref, out_ref, coef_ref, *, strip, band, samples):
+def render_kernel(sign_ref, packed_ref, out_ref, coef_ref, *, strip, band, samples, tiles, depths):
     unpack(packed_ref, coef_ref)
     slots, zblocks, lanes = coef_ref.shape
     sign = sign_ref[...]
@@ -120,7 +129,7 @@
 
     def block(step, state):
         source = jnp.where(flipped, zblocks - 1 - step, step)
-        zb = zblocks - 1 - source
+        zb = listed_at(source % tiles, source // tiles, tiles, depths)
         a = [
             jnp.broadcast_to(coef_ref[k, pl.ds(zb, 1), :], (2 * EDGE, lanes)) for k in range(slots)
         ]
@@ -188,7 +197,7 @@
     outgoing, sign = pl.pallas_call(
         lambda *refs: pack_kernel(*refs, tiles=tiles, depths=depths),
         out_shape=[
-            jax.ShapeDtypeStruct((depths, tiles, 5, 1, lanes), jnp.float32),
+            jax.ShapeDtypeStruct((zblocks, 5, 1, lanes), jnp.float32),
             jax.ShapeDtypeStruct((2 * EDGE, lanes), jnp.float32),
         ],
         in_specs=[pl.BlockSpec(memory_space=pltpu.SMEM)] + [pl.BlockSpec(memory_space=pltpu.HBM)] * 2,
@@ -197,25 +206,27 @@
             pltpu.VMEM((slots, columns, rows), jnp.float32),
             pltpu.VMEM((columns, rows), jnp.int32),
             pltpu.VMEM((depths, 5, tiles, lanes), jnp.float32),
-            pltpu.SemaphoreType.DMA((1 + slots,)),
+            pltpu.SemaphoreType.DMA((2,)),
         ],
         compiler_params=params,
         name="pack",
     )(view_flip, *(pltpu.with_memory_space_constraint(x, pltpu.HBM) for x in inputs))
-    sent = outgoing.reshape(zblocks, 5, 1, lanes)
-    falling = [list(range(zblocks - 1, -1, -1))]
+    devices = [(t, d) for d in range(depths) for t in range(tiles)]
+    listed = sorted(range(zblocks), key=lambda i: listed_at(*devices[i], tiles, depths))
     arrived = lax.all_to_all(
-        sent, ("depth", "tile"), split_axis=0, concat_axis=0, tiled=True, axis_index_groups=falling
+        outgoing, ("depth", "tile"), split_axis=0, concat_axis=0, tiled=True, axis_index_groups=[listed]
     )
     return pl.pallas_call(
-        lambda *refs: render_kernel(*refs, strip=strip, band=band, samples=EDGE * zblocks),
+        lambda *refs: render_kernel(
+            *refs, strip=strip, band=band, samples=EDGE * zblocks, tiles=tiles, depths=depths
+        ),
         out_shape=jax.ShapeDtypeStruct((4, strip * EDGE, band * EDGE), jnp.float32),
         in_specs=[vmem, vmem],
         out_specs=vmem,
         scratch_shapes=[pltpu.VMEM((slots, zblocks, lanes), jnp.float32)],
         compiler_params=params,
         name="render",
-    )(sign, arrived.reshape(outgoing.shape))
+    )(sign, arrived)
 
 
 def solution(mesh):

time: 18.7 us -> 18.5 us (0.989); the launches traced: 18.3 us -> 18.3 us
  no operation moved by 1% of the time
where the time goes in v6:
time: 18.5 us; the launch traced here: 18.3 us
  blocking collectives  14.6 us (79%)
  Pallas kernels  3.08 us (17%)
  between operations  0.66 us (4%)
    all_to_all x1, blocking collectives, per_device(): lax.all_to_all(outgoing, ('depth', 'tile'), split_axis=0, concat_axis=0,...  14.6 us
    pallas_call x1, Pallas kernels, per_device(): pl.pallas_call(lambda *refs: render_kernel(*refs, strip=strip, band=band,...  1.88 us
    pallas_call x1, Pallas kernels, per_device(): pl.pallas_call(lambda *refs: pack_kernel(*refs, tiles=tiles, depths=depth...  1.19 us

profile of v6, /device:TPU:0, one launch (start us, length us, event | category | flops | bytes accessed | tf_op | source)
XLA Modules:
  0.0 18.3 jit_solution(6604413457669552986)
XLA Ops:
  0.7 1.2 %pack.1 = (f32[32,5,1,128]{3,2,1,0:T(1,128)S(1)}, f32[8,128]{1,0:T(8,128)S(1)}) custom-call(s32[1]{0:T(128)S(6)} %copy.4.refs_0_, f32[8,32,128]{2,1,0:T(8,128)} %bitcast.2, s32[32,128]{1,0:T(8,128)} %bitcast.3), custom_call_target="tpu_custom_call" | custom-call | tf_op jit(solution)/shard_map/pack/pallas_call | solution.py:197
  1.9 14.6 %all_to_all.5.refs_1_ = f32[32,5,1,128]{3,2,1,0:T(1,128)S(1)} all-to-all(f32[32,5,1,128]{3,2,1,0:T(1,128)S(1)} %get-tuple-element.8), channel_id=1, replica_groups={{31,27,23,19,15,11,7,3,29,25,21,17,13,9,5,1,30,26,22,18,14,10,6,2,28,24..., dimensions={0} | all-to-all | bytes 163840 | tf_op jit(solution)/shard_map/all_to_all | solution.py:216
  16.5 1.9 %render.1 = f32[4,16,128]{2,1,0:T(8,128)} custom-call(f32[8,128]{1,0:T(8,128)S(1)} %get-tuple-element.7.refs_0_, f32[32,5,1,128]{3,2,1,0:T(1,128)S(1)} %all_to_all.5.refs_1_), custom_call_target="tpu_custom_call" | custom-call | tf_op jit(solution)/shard_map/render/pallas_call | solution.py:219

commit v7 on v6

--- a/solution.py
+++ b/solution.py
@@ -161,7 +161,7 @@
     zero = jnp.zeros((2 * EDGE, lanes), jnp.float32)
     one = jnp.ones((2 * EDGE, lanes), jnp.float32)
     start = (zero, one, zero, zero, zero)
-    state = lax.fori_loop(0, zblocks, block, (start, start), unroll=16)
+    state = lax.fori_loop(0, zblocks, block, (start, start), unroll=32)
 
     width = band * EDGE
     pick = lax.broadcasted_iota(jnp.int32, (2 * EDGE, width), 1)

time: 18.5 us -> 18.7 us (1.011)
  no operation moved by 1% of the time
where the time goes in v7:
time: 18.7 us; the launch traced here: 18.5 us
  blocking collectives  14.6 us (78%)
  Pallas kernels  3.26 us (17%)
  between operations  0.66 us (4%)
    all_to_all x1, blocking collectives, per_device(): lax.all_to_all(outgoing, ('depth', 'tile'), split_axis=0, concat_axis=0,...  14.6 us
    pallas_call x1, Pallas kernels, per_device(): pl.pallas_call(lambda *refs: render_kernel(*refs, strip=strip, band=band,...  2.07 us
    pallas_call x1, Pallas kernels, per_device(): pl.pallas_call(lambda *refs: pack_kernel(*refs, tiles=tiles, depths=depth...  1.19 us

profile of v7, /device:TPU:0, one launch (start us, length us, event | category | flops | bytes accessed | tf_op | source)
XLA Modules:
  0.0 18.5 jit_solution(161921387150255483)
XLA Ops:
  0.7 1.2 %pack.1 = (f32[32,5,1,128]{3,2,1,0:T(1,128)S(1)}, f32[8,128]{1,0:T(8,128)S(1)}) custom-call(s32[1]{0:T(128)S(6)} %copy.4.refs_0_, f32[8,32,128]{2,1,0:T(8,128)} %bitcast.2, s32[32,128]{1,0:T(8,128)} %bitcast.3), custom_call_target="tpu_custom_call" | custom-call | tf_op jit(solution)/shard_map/pack/pallas_call | solution.py:197
  1.9 14.6 %all_to_all.5.refs_1_ = f32[32,5,1,128]{3,2,1,0:T(1,128)S(1)} all-to-all(f32[32,5,1,128]{3,2,1,0:T(1,128)S(1)} %get-tuple-element.8), channel_id=1, replica_groups={{31,27,23,19,15,11,7,3,29,25,21,17,13,9,5,1,30,26,22,18,14,10,6,2,28,24..., dimensions={0} | all-to-all | bytes 163840 | tf_op jit(solution)/shard_map/all_to_all | solution.py:216
  16.5 2.1 %render.1 = f32[4,16,128]{2,1,0:T(8,128)} custom-call(f32[8,128]{1,0:T(8,128)S(1)} %get-tuple-element.7.refs_0_, f32[32,5,1,128]{3,2,1,0:T(1,128)S(1)} %all_to_all.5.refs_1_), custom_call_target="tpu_custom_call" | custom-call | tf_op jit(solution)/shard_map/render/pallas_call | solution.py:219

commit v8 on v7

--- a/solution.py
+++ b/solution.py
@@ -82,9 +82,9 @@
 
 
 def unpack(packed_ref, coef_ref):
-    zblocks, _, _, lanes = packed_ref.shape
+    zblocks, lanes = packed_ref.shape[0] // 5, packed_ref.shape[1]
     first = lax.broadcasted_iota(jnp.int32, (zblocks, lanes), 1) < lanes // 2
-    row = [packed_ref[:, q, 0, :] for q in range(5)]
+    row = [packed_ref[pl.ds(q, zblocks, stride=5), :] for q in range(5)]
     turned = [None] + [swap_halves(row[q]) for q in (1, 2, 3, 4)]
     keep = jnp.where(first, turned[4], 9.0 - row[4])
     slot = [row[0]] + [jnp.where(keep > q, row[q], 0.0) for q in (1, 2, 3)]
@@ -94,7 +94,7 @@
         coef_ref[k] = slot[k]
 
 
-def render_kernel(sign_ref, packed_ref, out_ref, coef_ref, *, strip, band, samples, tiles, depths):
+def render_kernel(sign_ref, packed_ref, out_ref, coef_ref, sampled_ref, *, strip, band, samples, tiles, depths):
     unpack(packed_ref, coef_ref)
     slots, zblocks, lanes = coef_ref.shape
     sign = sign_ref[...]
@@ -127,7 +127,7 @@
     blue_factor = blue_one * math.exp(-1.5)
     fade = -1.5 / samples
 
-    def block(step, state):
+    def factors(step):
         source = jnp.where(flipped, zblocks - 1 - step, step)
         zb = listed_at(source % tiles, source // tiles, tiles, depths)
         a = [
@@ -137,31 +137,49 @@
         odd = a[1] * c_y1 + a[5] * c_xy
         g_even = a[3] * c_z
         g_odd = a[7] * c_zy
-        halves = []
+        result = []
         for h in range(2):
-            depth, before, red, green, blue = state[h]
             base = even + odd if h == 0 else even - odd
             g = g_even + g_odd if h == 0 else g_even - g_odd
             near = g * ratio
             for f in (base + g, base + near, base - near, base - g):
                 v = jnp.exp2(f)
                 one_u = 1.0 + v * v
-                depth = depth + jnp.log2(one_u)
-                after = jnp.exp2(fade * depth)
-                weight = before - after
-                before = after
                 blue_u = blue_one + blue_factor * v
-                shared = weight / (one_u * blue_u)
-                red = red + shared * blue_u
-                green = green + weight * jnp.exp2(f * (f * (-1.0 / LOG2E)))
-                blue = blue + shared * one_u
-            halves.append((depth, before, red, green, blue))
-        return tuple(halves)
+                both = 1.0 / (one_u * blue_u)
+                green = jnp.exp2(f * (f * (-1.0 / LOG2E)))
+                result.append((jnp.log2(one_u), both * blue_u, green, both * one_u))
+        return result
+
+    blocks = 2 if zblocks % 2 == 0 else 1
+    sampled_ref[...] = jnp.zeros_like(sampled_ref)
+
+    def trip(number, state):
+        state = [list(part) for part in state]
+        for b in range(blocks):
+            for h in range(2):
+                depth, before, red, green, blue = state[h]
+                for z in range(EDGE):
+                    i = (b * 2 + h) * EDGE + z
+                    depth = depth + sampled_ref[0, i]
+                    after = jnp.exp2(fade * depth)
+                    weight = before - after
+                    before = after
+                    red = red + weight * sampled_ref[1, i]
+                    green = green + weight * sampled_ref[2, i]
+                    blue = blue + weight * sampled_ref[3, i]
+                state[h] = (depth, before, red, green, blue)
+        for b in range(blocks):
+            step = jnp.minimum(number * blocks + b, zblocks - 1)
+            for i, sample in enumerate(factors(step)):
+                for kind in range(4):
+                    sampled_ref[kind, b * 2 * EDGE + i] = sample[kind]
+        return tuple(tuple(part) for part in state)
 
     zero = jnp.zeros((2 * EDGE, lanes), jnp.float32)
     one = jnp.ones((2 * EDGE, lanes), jnp.float32)
     start = (zero, one, zero, zero, zero)
-    state = lax.fori_loop(0, zblocks, block, (start, start), unroll=32)
+    state = lax.fori_loop(0, zblocks // blocks + 1, trip, (start, start))
 
     width = band * EDGE
     pick = lax.broadcasted_iota(jnp.int32, (2 * EDGE, width), 1)
@@ -223,10 +241,13 @@
         out_shape=jax.ShapeDtypeStruct((4, strip * EDGE, band * EDGE), jnp.float32),
         in_specs=[vmem, vmem],
         out_specs=vmem,
-        scratch_shapes=[pltpu.VMEM((slots, zblocks, lanes), jnp.float32)],
+        scratch_shapes=[
+            pltpu.VMEM((slots, zblocks, lanes), jnp.float32),
+            pltpu.VMEM((4, 4 * EDGE, 2 * EDGE, lanes), jnp.float32),
+        ],
         compiler_params=params,
         name="render",
-    )(sign, arrived)
+    )(sign, arrived.reshape(zblocks * 5, lanes))
 
 
 def solution(mesh):

time: 18.7 us -> 19 us (1.016)
  Pallas kernels: 3.26 us -> 3.54 us
    pallas_call x1, Pallas kernels: 2.07 us -> 2.35 us  [per_device(): pl.pallas_call(lambda *refs: render_kernel(*refs, strip=strip, band=band,...]
where the time goes in v8:
time: 19 us; the launch traced here: 18.8 us
  blocking collectives  14.6 us (77%)
  Pallas kernels  3.54 us (19%)
  between operations  0.66 us (3%)
    all_to_all x1, blocking collectives, per_device(): lax.all_to_all(outgoing, ('depth', 'tile'), split_axis=0, concat_axis=0,...  14.6 us
    pallas_call x1, Pallas kernels, per_device(): pl.pallas_call(lambda *refs: render_kernel(*refs, strip=strip, band=band,...  2.35 us
    pallas_call x1, Pallas kernels, per_device(): pl.pallas_call(lambda *refs: pack_kernel(*refs, tiles=tiles, depths=depth...  1.19 us

profile of v8, /device:TPU:0, one launch (start us, length us, event | category | flops | bytes accessed | tf_op | source)
XLA Modules:
  0.0 18.8 jit_solution(8702345280727849789)
XLA Ops:
  0.7 1.2 %pack.1 = (f32[32,5,1,128]{3,2,1,0:T(1,128)S(1)}, f32[8,128]{1,0:T(8,128)S(1)}) custom-call(s32[1]{0:T(128)S(6)} %copy.4.refs_0_, f32[8,32,128]{2,1,0:T(8,128)} %bitcast.4, s32[32,128]{1,0:T(8,128)} %bitcast.5), custom_call_target="tpu_custom_call" | custom-call | tf_op jit(solution)/shard_map/pack/pallas_call | solution.py:215
  1.9 14.6 %all_to_all.5 = f32[32,5,1,128]{3,2,1,0:T(1,128)S(1)} all-to-all(f32[32,5,1,128]{3,2,1,0:T(1,128)S(1)} %get-tuple-element.8), channel_id=1, replica_groups={{31,27,23,19,15,11,7,3,29,25,21,17,13,9,5,1,30,26,22,18,14,10,6,2,28,24..., dimensions={0} | all-to-all | bytes 163840 | tf_op jit(solution)/shard_map/all_to_all | solution.py:234
  16.5 2.3 %render.1 = f32[4,16,128]{2,1,0:T(8,128)} custom-call(f32[8,128]{1,0:T(8,128)S(1)} %get-tuple-element.7.refs_0_, f32[160,128]{1,0:T(8,128)S(1)} %bitcast.3), custom_call_target="tpu_custom_call" | custom-call | tf_op jit(solution)/shard_map/render/pallas_call | solution.py:237

commit v9 on v6

--- a/solution.py
+++ b/solution.py
@@ -82,9 +82,9 @@
 
 
 def unpack(packed_ref, coef_ref):
-    zblocks, _, _, lanes = packed_ref.shape
+    zblocks, lanes = packed_ref.shape[0] // 5, packed_ref.shape[1]
     first = lax.broadcasted_iota(jnp.int32, (zblocks, lanes), 1) < lanes // 2
-    row = [packed_ref[:, q, 0, :] for q in range(5)]
+    row = [packed_ref[pl.ds(q, zblocks, stride=5), :] for q in range(5)]
     turned = [None] + [swap_halves(row[q]) for q in (1, 2, 3, 4)]
     keep = jnp.where(first, turned[4], 9.0 - row[4])
     slot = [row[0]] + [jnp.where(keep > q, row[q], 0.0) for q in (1, 2, 3)]
@@ -213,8 +213,9 @@
     )(view_flip, *(pltpu.with_memory_space_constraint(x, pltpu.HBM) for x in inputs))
     devices = [(t, d) for d in range(depths) for t in range(tiles)]
     listed = sorted(range(zblocks), key=lambda i: listed_at(*devices[i], tiles, depths))
+    chunks = outgoing.reshape(zblocks, 1, 5 * lanes)
     arrived = lax.all_to_all(
-        outgoing, ("depth", "tile"), split_axis=0, concat_axis=0, tiled=True, axis_index_groups=[listed]
+        chunks, ("depth", "tile"), split_axis=0, concat_axis=0, tiled=True, axis_index_groups=[listed]
     )
     return pl.pallas_call(
         lambda *refs: render_kernel(
@@ -226,7 +227,7 @@
         scratch_shapes=[pltpu.VMEM((slots, zblocks, lanes), jnp.float32)],
         compiler_params=params,
         name="render",
-    )(sign, arrived)
+    )(sign, arrived.reshape(zblocks * 5, lanes))
 
 
 def solution(mesh):

time: 18.5 us -> 18.5 us (level)
  no operation moved by 1% of the time
where the time goes in v9:
time: 18.5 us; the launch traced here: 18.3 us
  blocking collectives  14.6 us (79%)
  Pallas kernels  3.08 us (17%)
  between operations  0.66 us (4%)
    all_to_all x1, blocking collectives, per_device(): lax.all_to_all(chunks, ('depth', 'tile'), split_axis=0, concat_axis=0, ti...  14.6 us
    pallas_call x1, Pallas kernels, per_device(): pl.pallas_call(lambda *refs: render_kernel(*refs, strip=strip, band=band,...  1.88 us
    pallas_call x1, Pallas kernels, per_device(): pl.pallas_call(lambda *refs: pack_kernel(*refs, tiles=tiles, depths=depth...  1.19 us

profile of v9, /device:TPU:0, one launch (start us, length us, event | category | flops | bytes accessed | tf_op | source)
XLA Modules:
  0.0 18.3 jit_solution(16303356504525048499)
XLA Ops:
  0.7 1.2 %pack.1 = (f32[32,5,1,128]{3,2,1,0:T(1,128)S(1)}, f32[8,128]{1,0:T(8,128)S(1)}) custom-call(s32[1]{0:T(128)S(6)} %copy.5.refs_0_, f32[8,32,128]{2,1,0:T(8,128)} %bitcast.6, s32[32,128]{1,0:T(8,128)} %bitcast.7), custom_call_target="tpu_custom_call" | custom-call | tf_op jit(solution)/shard_map/pack/pallas_call | solution.py:197
  1.9 14.6 %all_to_all.5 = f32[32,1,640]{2,1,0:T(1,128)S(1)} all-to-all(f32[32,1,640]{2,1,0:T(1,128)S(1)} %bitcast.5), channel_id=1, replica_groups={{31,27,23,19,15,11,7,3,29,25,21,17,13,9,5,1,30,26,22,18,14,10,6,2,28,24..., dimensions={0} | all-to-all | bytes 163840 | tf_op jit(solution)/shard_map/all_to_all | solution.py:217
  16.5 1.9 %render.1 = f32[4,16,128]{2,1,0:T(8,128)} custom-call(f32[8,128]{1,0:T(8,128)S(1)} %get-tuple-element.7.refs_0_, f32[160,128]{1,0:T(8,128)S(1)} %bitcast.4), custom_call_target="tpu_custom_call" | custom-call | tf_op jit(solution)/shard_map/render/pallas_call | solution.py:220

commit v10 on v9

--- a/solution.py
+++ b/solution.py
@@ -39,7 +39,7 @@
     _, columns, rows = coef_ref.shape
     strip = columns // tiles
     band = rows // depths
-    moves = ((coef_hbm, coef_ref), (keep_hbm, keep_ref))
+    moves = [(coef_hbm.at[pl.ds(k, 4)], coef_ref.at[pl.ds(k, 4)]) for k in (0, 4)] + [(keep_hbm, keep_ref)]
     fetches = [pltpu.make_async_copy(a, b, arrival.at[i]) for i, (a, b) in enumerate(moves)]
     for fetch in fetches:
         fetch.start()
@@ -161,7 +161,7 @@
     zero = jnp.zeros((2 * EDGE, lanes), jnp.float32)
     one = jnp.ones((2 * EDGE, lanes), jnp.float32)
     start = (zero, one, zero, zero, zero)
-    state = lax.fori_loop(0, zblocks, block, (start, start), unroll=16)
+    state = lax.fori_loop(0, zblocks, block, (start, start), unroll=8)
 
     width = band * EDGE
     pick = lax.broadcasted_iota(jnp.int32, (2 * EDGE, width), 1)
@@ -206,7 +206,7 @@
             pltpu.VMEM((slots, columns, rows), jnp.float32),
             pltpu.VMEM((columns, rows), jnp.int32),
             pltpu.VMEM((depths, 5, tiles, lanes), jnp.float32),
-            pltpu.SemaphoreType.DMA((2,)),
+            pltpu.SemaphoreType.DMA((3,)),
         ],
         compiler_params=params,
         name="pack",

time: 18.5 us -> 18.6 us (level)
  no operation moved by 1% of the time
where the time goes in v10:
time: 18.6 us; the launch traced here: 18.4 us
  blocking collectives  14.6 us (78%)
  Pallas kernels  3.13 us (17%)
  between operations  0.66 us (4%)
    all_to_all x1, blocking collectives, per_device(): lax.all_to_all(chunks, ('depth', 'tile'), split_axis=0, concat_axis=0, ti...  14.6 us
    pallas_call x1, Pallas kernels, per_device(): pl.pallas_call(lambda *refs: render_kernel(*refs, strip=strip, band=band,...  1.96 us
    pallas_call x1, Pallas kernels, per_device(): pl.pallas_call(lambda *refs: pack_kernel(*refs, tiles=tiles, depths=depth...  1.17 us

profile of v10, /device:TPU:0, one launch (start us, length us, event | category | flops | bytes accessed | tf_op | source)
XLA Modules:
  0.0 18.4 jit_solution(15692641603367007577)
XLA Ops:
  0.7 1.2 %pack.1 = (f32[32,5,1,128]{3,2,1,0:T(1,128)S(1)}, f32[8,128]{1,0:T(8,128)S(1)}) custom-call(s32[1]{0:T(128)S(6)} %copy.5.refs_0_, f32[8,32,128]{2,1,0:T(8,128)} %bitcast.6, s32[32,128]{1,0:T(8,128)} %bitcast.7), custom_call_target="tpu_custom_call" | custom-call | tf_op jit(solution)/shard_map/pack/pallas_call | solution.py:197
  1.8 14.6 %all_to_all.5 = f32[32,1,640]{2,1,0:T(1,128)S(1)} all-to-all(f32[32,1,640]{2,1,0:T(1,128)S(1)} %bitcast.5), channel_id=1, replica_groups={{31,27,23,19,15,11,7,3,29,25,21,17,13,9,5,1,30,26,22,18,14,10,6,2,28,24..., dimensions={0} | all-to-all | bytes 163840 | tf_op jit(solution)/shard_map/all_to_all | solution.py:217
  16.4 2.0 %render.1 = f32[4,16,128]{2,1,0:T(8,128)} custom-call(f32[8,128]{1,0:T(8,128)S(1)} %get-tuple-element.7.refs_0_, f32[160,128]{1,0:T(8,128)S(1)} %bitcast.4), custom_call_target="tpu_custom_call" | custom-call | tf_op jit(solution)/shard_map/render/pallas_call | solution.py:220

commit v11 on v10

--- a/solution.py
+++ b/solution.py
@@ -81,7 +81,7 @@
             out_ref[listed_at(t, d, tiles, depths), :, 0, :] = rows_ref[d, :, t, :]
 
 
-def unpack(packed_ref, coef_ref):
+def unpack(packed_ref, coef_ref, scales):
     zblocks, lanes = packed_ref.shape[0] // 5, packed_ref.shape[1]
     first = lax.broadcasted_iota(jnp.int32, (zblocks, lanes), 1) < lanes // 2
     row = [packed_ref[pl.ds(q, zblocks, stride=5), :] for q in range(5)]
@@ -91,15 +91,16 @@
     slot.append(jnp.where(keep > 4, jnp.where(first, row[4], turned[4]), 0.0))
     slot += [jnp.where(keep > k, turned[8 - k], 0.0) for k in (5, 6, 7)]
     for k in range(8):
-        coef_ref[k] = slot[k]
+        coef_ref[k] = slot[k] * scales[k] if k in scales else slot[k]
 
 
 def render_kernel(sign_ref, packed_ref, out_ref, coef_ref, *, strip, band, samples, tiles, depths):
-    unpack(packed_ref, coef_ref)
     slots, zblocks, lanes = coef_ref.shape
     sign = sign_ref[...]
     flipped = jnp.max(sign) < 0.0
     b1 = [cosine(1, i) for i in range(EDGE)]
+    c_z = 0.25 * LOG2E * b1[0]
+    unpack(packed_ref, coef_ref, {0: 0.125 * LOG2E, 3: c_z * sign[:1]})
     row = lax.broadcasted_iota(jnp.int32, (2 * EDGE, lanes), 0)
     x = row % EDGE
     y = row // EDGE
@@ -114,17 +115,14 @@
     x2 = table(x, [cosine(2, i) for i in range(EDGE)])
     y1 = table(y, b1[:2])
     y2 = table(y, [cosine(2, i) for i in range(2)])
-    c_dc = 0.125 * LOG2E
     c_x1 = (0.25 * LOG2E) * x1
     c_x2 = (0.25 * LOG2E) * x2
     c_y1 = (0.25 * LOG2E) * y1
     c_y2 = (0.25 * LOG2E) * y2
     c_xy = (0.5 * LOG2E) * x1 * y1
-    c_z = jnp.full((2 * EDGE, lanes), 0.25 * LOG2E * b1[0], jnp.float32) * sign
     c_zy = (0.5 * LOG2E * b1[0]) * y1 * sign
     ratio = b1[1] / b1[0]
-    blue_one = 2.0**-20
-    blue_factor = blue_one * math.exp(-1.5)
+    blue_factor = math.exp(-1.5)
     fade = -1.5 / samples
 
     def block(step, state):
@@ -133,9 +131,9 @@
         a = [
             jnp.broadcast_to(coef_ref[k, pl.ds(zb, 1), :], (2 * EDGE, lanes)) for k in range(slots)
         ]
-        even = a[0] * c_dc + a[2] * c_x1 + a[4] * c_y2 + a[6] * c_x2
+        even = a[0] + a[2] * c_x1 + a[4] * c_y2 + a[6] * c_x2
         odd = a[1] * c_y1 + a[5] * c_xy
-        g_even = a[3] * c_z
+        g_even = a[3]
         g_odd = a[7] * c_zy
         halves = []
         for h in range(2):
@@ -150,18 +148,16 @@
                 after = jnp.exp2(fade * depth)
                 weight = before - after
                 before = after
-                blue_u = blue_one + blue_factor * v
-                shared = weight / (one_u * blue_u)
-                red = red + shared * blue_u
+                red = red + weight / one_u
                 green = green + weight * jnp.exp2(f * (f * (-1.0 / LOG2E)))
-                blue = blue + shared * one_u
+                blue = blue + weight / (1.0 + blue_factor * v)
             halves.append((depth, before, red, green, blue))
         return tuple(halves)
 
     zero = jnp.zeros((2 * EDGE, lanes), jnp.float32)
     one = jnp.ones((2 * EDGE, lanes), jnp.float32)
     start = (zero, one, zero, zero, zero)
-    state = lax.fori_loop(0, zblocks, block, (start, start), unroll=8)
+    state = lax.fori_loop(0, zblocks, block, (start, start), unroll=16)
 
     width = band * EDGE
     pick = lax.broadcasted_iota(jnp.int32, (2 * EDGE, width), 1)
@@ -171,7 +167,7 @@
     outs = []
     for _, before, red, green, blue in state:
         opacity = 1.0 - before
-        outs.append((opacity - red, green, blue * blue_one, opacity))
+        outs.append((opacity - red, green, blue, opacity))
     for ch in range(4):
         for b in range(strip):
             index = place + b * (band // 2)

time: 18.6 us -> 18.5 us (level)
  no operation moved by 1% of the time
where the time goes in v11:
time: 18.5 us; the launch traced here: 18.3 us
  blocking collectives  14.6 us (79%)
  Pallas kernels  3.05 us (16%)
  between operations  0.66 us (4%)
    all_to_all x1, blocking collectives, per_device(): lax.all_to_all(chunks, ('depth', 'tile'), split_axis=0, concat_axis=0, ti...  14.6 us
    pallas_call x1, Pallas kernels, per_device(): pl.pallas_call(lambda *refs: render_kernel(*refs, strip=strip, band=band,...  1.88 us
    pallas_call x1, Pallas kernels, per_device(): pl.pallas_call(lambda *refs: pack_kernel(*refs, tiles=tiles, depths=depth...  1.17 us

profile of v11, /device:TPU:0, one launch (start us, length us, event | category | flops | bytes accessed | tf_op | source)
XLA Modules:
  0.0 18.3 jit_solution(377281261237514775)
XLA Ops:
  0.7 1.2 %pack.1 = (f32[32,5,1,128]{3,2,1,0:T(1,128)S(1)}, f32[8,128]{1,0:T(8,128)S(1)}) custom-call(s32[1]{0:T(128)S(6)} %copy.5.refs_0_, f32[8,32,128]{2,1,0:T(8,128)} %bitcast.6, s32[32,128]{1,0:T(8,128)} %bitcast.7), custom_call_target="tpu_custom_call" | custom-call | tf_op jit(solution)/shard_map/pack/pallas_call | solution.py:193
  1.8 14.6 %all_to_all.5 = f32[32,1,640]{2,1,0:T(1,128)S(1)} all-to-all(f32[32,1,640]{2,1,0:T(1,128)S(1)} %bitcast.5), channel_id=1, replica_groups={{31,27,23,19,15,11,7,3,29,25,21,17,13,9,5,1,30,26,22,18,14,10,6,2,28,24..., dimensions={0} | all-to-all | bytes 163840 | tf_op jit(solution)/shard_map/all_to_all | solution.py:213
  16.4 1.9 %render.1 = f32[4,16,128]{2,1,0:T(8,128)} custom-call(f32[8,128]{1,0:T(8,128)S(1)} %get-tuple-element.7.refs_0_, f32[160,128]{1,0:T(8,128)S(1)} %bitcast.4), custom_call_target="tpu_custom_call" | custom-call | tf_op jit(solution)/shard_map/render/pallas_call | solution.py:216

commit v12 on v9

--- a/solution.py
+++ b/solution.py
@@ -34,7 +34,7 @@
 
 
 def pack_kernel(
-    flip_ref, coef_hbm, keep_hbm, out_ref, sign_ref, coef_ref, keep_ref, rows_ref, arrival, *, tiles, depths
+    coef_hbm, keep_hbm, out_ref, coef_ref, keep_ref, rows_ref, arrival, *, tiles, depths
 ):
     _, columns, rows = coef_ref.shape
     strip = columns // tiles
@@ -62,7 +62,6 @@
             result.append(jnp.where(keep > q, slot[q], take(slot[8 - q], other)))
         result[4] = jnp.where(even, result[4], (9 - keep).astype(jnp.float32))
         packed.append(result)
-    sign_ref[...] = jnp.full(sign_ref.shape, 1 - 2 * flip_ref[0], jnp.int32).astype(jnp.float32)
     half = strip * band // 2
     parity = lane // half % 2
     column = lane // (band // 2) % strip
@@ -94,11 +93,11 @@
         coef_ref[k] = slot[k]
 
 
-def render_kernel(sign_ref, packed_ref, out_ref, coef_ref, *, strip, band, samples, tiles, depths):
+def render_kernel(flip_ref, packed_ref, out_ref, coef_ref, *, strip, band, samples, tiles, depths):
     unpack(packed_ref, coef_ref)
     slots, zblocks, lanes = coef_ref.shape
-    sign = sign_ref[...]
-    flipped = jnp.max(sign) < 0.0
+    flipped = flip_ref[0] > 0
+    sign = jnp.where(flipped, jnp.float32(-1.0), jnp.float32(1.0))
     b1 = [cosine(1, i) for i in range(EDGE)]
     row = lax.broadcasted_iota(jnp.int32, (2 * EDGE, lanes), 0)
     x = row % EDGE
@@ -194,14 +193,11 @@
     params = pltpu.CompilerParams(vmem_limit_bytes=8 * 1024 * 1024)
     lanes = strip * band
     inputs = (coefficients.reshape(slots, columns, rows), keep_count.reshape(columns, rows))
-    outgoing, sign = pl.pallas_call(
+    outgoing = pl.pallas_call(
         lambda *refs: pack_kernel(*refs, tiles=tiles, depths=depths),
-        out_shape=[
-            jax.ShapeDtypeStruct((zblocks, 5, 1, lanes), jnp.float32),
-            jax.ShapeDtypeStruct((2 * EDGE, lanes), jnp.float32),
-        ],
-        in_specs=[pl.BlockSpec(memory_space=pltpu.SMEM)] + [pl.BlockSpec(memory_space=pltpu.HBM)] * 2,
-        out_specs=[vmem, vmem],
+        out_shape=jax.ShapeDtypeStruct((zblocks, 5, 1, lanes), jnp.float32),
+        in_specs=[pl.BlockSpec(memory_space=pltpu.HBM)] * 2,
+        out_specs=vmem,
         scratch_shapes=[
             pltpu.VMEM((slots, columns, rows), jnp.float32),
             pltpu.VMEM((columns, rows), jnp.int32),
@@ -210,7 +206,7 @@
         ],
         compiler_params=params,
         name="pack",
-    )(view_flip, *(pltpu.with_memory_space_constraint(x, pltpu.HBM) for x in inputs))
+    )(*(pltpu.with_memory_space_constraint(x, pltpu.HBM) for x in inputs))
     devices = [(t, d) for d in range(depths) for t in range(tiles)]
     listed = sorted(range(zblocks), key=lambda i: listed_at(*devices[i], tiles, depths))
     chunks = outgoing.reshape(zblocks, 1, 5 * lanes)
@@ -222,12 +218,12 @@
             *refs, strip=strip, band=band, samples=EDGE * zblocks, tiles=tiles, depths=depths
         ),
         out_shape=jax.ShapeDtypeStruct((4, strip * EDGE, band * EDGE), jnp.float32),
-        in_specs=[vmem, vmem],
+        in_specs=[pl.BlockSpec(memory_space=pltpu.SMEM), vmem],
         out_specs=vmem,
         scratch_shapes=[pltpu.VMEM((slots, zblocks, lanes), jnp.float32)],
         compiler_params=params,
         name="render",
-    )(sign, arrived.reshape(zblocks * 5, lanes))
+    )(view_flip, arrived.reshape(zblocks * 5, lanes))
 
 
 def solution(mesh):

time: 18.5 us -> 18.7 us (1.011)
  blocking collectives: 14.6 us -> 0 us
  starting transfers between devices: 0 us -> 7.3 us
  waiting for transfers between devices: 0 us -> 6.85 us
  Pallas kernels: 3.08 us -> 3.65 us
    all_to_all x1 -> x0, blocking collectives: 14.6 us -> none  [per_device(): lax.all_to_all(chunks, ('depth', 'tile'), split_axis=0, concat_axis=0, ti...]
    all_to_all x0 -> x1, starting transfers between devices: none -> 7.3 us  [per_device(): lax.all_to_all(chunks, ('depth', 'tile'), split_axis=0, concat_axis=0, ti...]
    all_to_all x0 -> x1, waiting for transfers between devices: none -> 6.85 us  [per_device(): lax.all_to_all(chunks, ('depth', 'tile'), split_axis=0, concat_axis=0, ti...]
    pallas_call x1, Pallas kernels: 1.19 us -> 1.81 us  [per_device(): pl.pallas_call(lambda *refs: pack_kernel(*refs, tiles=tiles, depths=depth...]
  transfers between devices with their start and end apart: 0 -> 1, of which waited for: 0 -> 1; matrix products, arithmetic and copies ran while one was open for 0% -> 0% of each run, Pallas kernels for 0% -> 0%
where the time goes in v12:
time: 18.7 us; the launch traced here: 18.5 us
  starting transfers between devices  7.3 us (39%)
  waiting for transfers between devices  6.85 us (37%)
  Pallas kernels  3.65 us (20%)
  between operations  0.66 us (4%)
    all_to_all x1, starting transfers between devices, per_device(): lax.all_to_all(chunks, ('depth', 'tile'), split_axis=0, concat_axis=0, ti...  7.3 us
    all_to_all x1, waiting for transfers between devices, per_device(): lax.all_to_all(chunks, ('depth', 'tile'), split_axis=0, concat_axis=0, ti...  6.85 us
    pallas_call x1, Pallas kernels, per_device(): pl.pallas_call(lambda *refs: render_kernel(*refs, strip=strip, band=band,...  1.84 us
    pallas_call x1, Pallas kernels, per_device(): pl.pallas_call(lambda *refs: pack_kernel(*refs, tiles=tiles, depths=depth...  1.81 us
  transfers between devices with their start and end apart: 1, of which 1 were waited for; matrix products, arithmetic and copies ran while one was open for 0% of the time, Pallas kernels for 0%

profile of v12, /device:TPU:0, one launch (start us, length us, event | category | flops | bytes accessed | tf_op | source)
XLA Modules:
  0.0 18.5 jit_solution(7234192425378514131)
XLA Ops:
  0.0 1.8 %pack.1 = f32[32,5,1,128]{3,2,1,0:T(1,128)} custom-call(f32[8,32,128]{2,1,0:T(8,128)} %bitcast.5, s32[32,128]{1,0:T(8,128)} %bitcast.6), custom_call_target="tpu_custom_call" | custom-call | tf_op jit(solution)/shard_map/pack/pallas_call | solution.py:196
  1.8 7.3 %all-to-all-start = ((f32[32,1,640]{2,1,0:T(1,128)}), f32[32,1,640]{2,1,0:T(1,128)S(1)}, u32[]{:S(2)}, u32[]{:S(2)}) async-start(f32[32,1,640]{2,1,0:T(1,128)} %bitcast.2), calls=%async_computation | async-start | bytes 163840 | tf_op jit(solution)/shard_map/all_to_all | solution.py:213
  9.8 6.8 %all-to-all-done = f32[32,1,640]{2,1,0:T(1,128)S(1)} async-done(((f32[32,1,640]{2,1,0:T(1,128)}), f32[32,1,640]{2,1,0:T(1,128)S(1)}, u32[]{:S(2)}, u32[]{:S(2)}) %all-to-all-start) | async-done | bytes 81952 | tf_op jit(solution)/shard_map/all_to_all | solution.py:213
  16.6 1.8 %render.1 = f32[4,16,128]{2,1,0:T(8,128)} custom-call(s32[1]{0:T(128)S(6)} %copy.5.refs_0_, f32[160,128]{1,0:T(8,128)S(1)} %bitcast.4), custom_call_target="tpu_custom_call" | custom-call | tf_op jit(solution)/shard_map/render/pallas_call | solution.py:216
Async XLA Ops:
  1.8 14.8 %all-to-all-start = ((f32[32,1,640]{2,1,0:T(1,128)}), f32[32,1,640]{2,1,0:T(1,128)S(1)}, u32[]{:S(2)}, u32[]{:S(2)}) async-start(f32[32,1,640]{2,1,0:T(1,128)} %bitcast.2), calls=%async_computation | async-start | bytes 163840 | tf_op jit(solution)/shard_map/all_to_all | solution.py:213

commit v13 on v9

--- a/solution.py
+++ b/solution.py
@@ -94,11 +94,13 @@
         coef_ref[k] = slot[k]
 
 
-def render_kernel(sign_ref, packed_ref, out_ref, coef_ref, *, strip, band, samples, tiles, depths):
+def render_kernel(
+    flip_ref, sign_ref, packed_ref, out_hbm, coef_ref, out_ref, leaving, *, strip, band, samples, tiles, depths
+):
     unpack(packed_ref, coef_ref)
     slots, zblocks, lanes = coef_ref.shape
     sign = sign_ref[...]
-    flipped = jnp.max(sign) < 0.0
+    flipped = flip_ref[0] > 0
     b1 = [cosine(1, i) for i in range(EDGE)]
     row = lax.broadcasted_iota(jnp.int32, (2 * EDGE, lanes), 0)
     x = row % EDGE
@@ -172,6 +174,7 @@
     for _, before, red, green, blue in state:
         opacity = 1.0 - before
         outs.append((opacity - red, green, blue * blue_one, opacity))
+    copies = [pltpu.make_async_copy(out_ref.at[ch], out_hbm.at[ch], leaving.at[ch]) for ch in range(4)]
     for ch in range(4):
         for b in range(strip):
             index = place + b * (band // 2)
@@ -181,6 +184,9 @@
             first, second = both[:EDGE], both[EDGE:]
             use_first = (y_out[:EDGE] == 0) | (y_out[:EDGE] == 3)
             out_ref[ch, pl.ds(b * EDGE, EDGE), :] = jnp.where(use_first, first, second)
+        copies[ch].start()
+    for copy in copies:
+        copy.wait()
 
 
 def per_device(coefficients, keep_count, view_flip):
@@ -222,12 +228,16 @@
             *refs, strip=strip, band=band, samples=EDGE * zblocks, tiles=tiles, depths=depths
         ),
         out_shape=jax.ShapeDtypeStruct((4, strip * EDGE, band * EDGE), jnp.float32),
-        in_specs=[vmem, vmem],
-        out_specs=vmem,
-        scratch_shapes=[pltpu.VMEM((slots, zblocks, lanes), jnp.float32)],
+        in_specs=[pl.BlockSpec(memory_space=pltpu.SMEM), vmem, vmem],
+        out_specs=pl.BlockSpec(memory_space=pltpu.HBM),
+        scratch_shapes=[
+            pltpu.VMEM((slots, zblocks, lanes), jnp.float32),
+            pltpu.VMEM((4, strip * EDGE, band * EDGE), jnp.float32),
+            pltpu.SemaphoreType.DMA((4,)),
+        ],
         compiler_params=params,
         name="render",
-    )(sign, arrived.reshape(zblocks * 5, lanes))
+    )(view_flip, sign, arrived.reshape(zblocks * 5, lanes))
 
 
 def solution(mesh):

time: 18.5 us -> 18.5 us (level)
  no operation moved by 1% of the time
where the time goes in v13:
time: 18.5 us; the launch traced here: 18.3 us
  blocking collectives  14.6 us (79%)
  Pallas kernels  3.06 us (17%)
  between operations  0.66 us (4%)
    all_to_all x1, blocking collectives, per_device(): lax.all_to_all(chunks, ('depth', 'tile'), split_axis=0, concat_axis=0, ti...  14.6 us
    pallas_call x1, Pallas kernels, per_device(): pl.pallas_call(lambda *refs: render_kernel(*refs, strip=strip, band=band,...  1.87 us
    pallas_call x1, Pallas kernels, per_device(): pl.pallas_call(lambda *refs: pack_kernel(*refs, tiles=tiles, depths=depth...  1.19 us

profile of v13, /device:TPU:0, one launch (start us, length us, event | category | flops | bytes accessed | tf_op | source)
XLA Modules:
  0.0 18.3 jit_solution(16129325747655639820)
XLA Ops:
  0.7 1.2 %pack.1 = (f32[32,5,1,128]{3,2,1,0:T(1,128)S(1)}, f32[8,128]{1,0:T(8,128)S(1)}) custom-call(s32[1]{0:T(128)S(6)} %copy.5.refs_0_, f32[8,32,128]{2,1,0:T(8,128)} %bitcast.6, s32[32,128]{1,0:T(8,128)} %bitcast.7), custom_call_target="tpu_custom_call" | custom-call | tf_op jit(solution)/shard_map/pack/pallas_call | solution.py:203
  1.9 14.6 %all_to_all.5 = f32[32,1,640]{2,1,0:T(1,128)S(1)} all-to-all(f32[32,1,640]{2,1,0:T(1,128)S(1)} %bitcast.5), channel_id=1, replica_groups={{31,27,23,19,15,11,7,3,29,25,21,17,13,9,5,1,30,26,22,18,14,10,6,2,28,24..., dimensions={0} | all-to-all | bytes 163840 | tf_op jit(solution)/shard_map/all_to_all | solution.py:223
  16.5 1.9 %render.1 = f32[4,16,128]{2,1,0:T(8,128)} custom-call(s32[1]{0:T(128)S(6)} %copy.5.refs_0_, f32[8,128]{1,0:T(8,128)S(1)} %get-tuple-element.7.refs_1_, f32[160,128]{1,0:T(8,128)S(1)} %bitcast.4), custom_call_target="tpu_custom_call" | custom-call | tf_op jit(solution)/shard_map/render/pallas_call | solution.py:226

commit v14 on v13

--- a/solution.py
+++ b/solution.py
@@ -23,14 +23,14 @@
     return jnp.concatenate([values[:, half:], values[:, :half]], axis=1)
 
 
+def split(values, size):
+    if size & (size - 1):
+        return values // size, values % size
+    return values >> (size.bit_length() - 1), values & (size - 1)
+
+
 def listed_at(t, d, tiles, depths):
-    turned, size = 0, 1
-    while 2 * size <= depths:
-        turned = turned + d // size % 2 * (depths // (2 * size))
-        size *= 2
-    if size != depths:
-        turned = d
-    return tiles * depths - 1 - turned * tiles - t
+    return tiles * depths - 1 - d * tiles - t
 
 
 def pack_kernel(
@@ -46,12 +46,13 @@
     for fetch in fetches:
         fetch.wait()
     lane = lax.broadcasted_iota(jnp.int32, (tiles, rows), 1)
-    even = lane % 2 == 0
+    odd = split(lane, 2)[1]
+    even = odd == 0
 
     def take(values, index):
         return jnp.take_along_axis(values, index, axis=1)
 
-    other = lane + 1 - 2 * (lane % 2)
+    other = lane + 1 - 2 * odd
     packed = []
     for b in range(strip):
         mine = pl.ds(b, tiles, stride=strip)
@@ -64,9 +65,10 @@
         packed.append(result)
     sign_ref[...] = jnp.full(sign_ref.shape, 1 - 2 * flip_ref[0], jnp.int32).astype(jnp.float32)
     half = strip * band // 2
-    parity = lane // half % 2
-    column = lane // (band // 2) % strip
-    source = lane % (band // 2) * 2 + parity
+    chunk, within = split(lane, band // 2)
+    parity, column = split(chunk, strip)
+    parity = split(parity, 2)[1]
+    source = within * 2 + parity
     for d in range(depths):
         for q in range(5):
             gathered = [take(packed[b][q], source + d * band) for b in range(strip)]
@@ -95,7 +97,7 @@
 
 
 def render_kernel(
-    flip_ref, sign_ref, packed_ref, out_hbm, coef_ref, out_ref, leaving, *, strip, band, samples, tiles, depths
+    flip_ref, sign_ref, packed_ref, out_hbm, coef_ref, out_ref, leaving, *, strip, band, samples
 ):
     unpack(packed_ref, coef_ref)
     slots, zblocks, lanes = coef_ref.shape
@@ -103,8 +105,7 @@
     flipped = flip_ref[0] > 0
     b1 = [cosine(1, i) for i in range(EDGE)]
     row = lax.broadcasted_iota(jnp.int32, (2 * EDGE, lanes), 0)
-    x = row % EDGE
-    y = row // EDGE
+    y, x = split(row, EDGE)
 
     def table(position, values):
         result = jnp.full((2 * EDGE, lanes), values[0], jnp.float32)
@@ -131,7 +132,7 @@
 
     def block(step, state):
         source = jnp.where(flipped, zblocks - 1 - step, step)
-        zb = listed_at(source % tiles, source // tiles, tiles, depths)
+        zb = zblocks - 1 - source
         a = [
             jnp.broadcast_to(coef_ref[k, pl.ds(zb, 1), :], (2 * EDGE, lanes)) for k in range(slots)
         ]
@@ -167,9 +168,9 @@
 
     width = band * EDGE
     pick = lax.broadcasted_iota(jnp.int32, (2 * EDGE, width), 1)
-    y_out = pick % EDGE
-    place = pick // EDGE
-    place = place % 2 * (lanes // 2) + place // 2
+    place, y_out = split(pick, EDGE)
+    place, odd = split(place, 2)
+    place = odd * (lanes // 2) + place
     outs = []
     for _, before, red, green, blue in state:
         opacity = 1.0 - before
@@ -224,9 +225,7 @@
         chunks, ("depth", "tile"), split_axis=0, concat_axis=0, tiled=True, axis_index_groups=[listed]
     )
     return pl.pallas_call(
-        lambda *refs: render_kernel(
-            *refs, strip=strip, band=band, samples=EDGE * zblocks, tiles=tiles, depths=depths
-        ),
+        lambda *refs: render_kernel(*refs, strip=strip, band=band, samples=EDGE * zblocks),
         out_shape=jax.ShapeDtypeStruct((4, strip * EDGE, band * EDGE), jnp.float32),
         in_specs=[pl.BlockSpec(memory_space=pltpu.SMEM), vmem, vmem],
         out_specs=pl.BlockSpec(memory_space=pltpu.HBM),

time: 18.5 us -> 18.5 us (level)
  no operation moved by 1% of the time
where the time goes in v14:
time: 18.5 us; the launch traced here: 18.3 us
  blocking collectives  14.6 us (79%)
  Pallas kernels  3.02 us (16%)
  between operations  0.66 us (4%)
    all_to_all x1, blocking collectives, per_device(): lax.all_to_all(chunks, ('depth', 'tile'), split_axis=0, concat_axis=0, ti...  14.6 us
    pallas_call x1, Pallas kernels, per_device(): pl.pallas_call(lambda *refs: render_kernel(*refs, strip=strip, band=band,...  1.83 us
    pallas_call x1, Pallas kernels, per_device(): pl.pallas_call(lambda *refs: pack_kernel(*refs, tiles=tiles, depths=depth...  1.19 us

profile of v14, /device:TPU:0, one launch (start us, length us, event | category | flops | bytes accessed | tf_op | source)
XLA Modules:
  0.0 18.3 jit_solution(12542530708623130336)
XLA Ops:
  0.7 1.2 %pack.1 = (f32[32,5,1,128]{3,2,1,0:T(1,128)S(1)}, f32[8,128]{1,0:T(8,128)S(1)}) custom-call(s32[1]{0:T(128)S(6)} %copy.5.refs_0_, f32[8,32,128]{2,1,0:T(8,128)} %bitcast.6, s32[32,128]{1,0:T(8,128)} %bitcast.7), custom_call_target="tpu_custom_call" | custom-call | tf_op jit(solution)/shard_map/pack/pallas_call | solution.py:204
  1.9 14.6 %all_to_all.5 = f32[32,1,640]{2,1,0:T(1,128)S(1)} all-to-all(f32[32,1,640]{2,1,0:T(1,128)S(1)} %bitcast.5), channel_id=1, replica_groups={{31,27,23,19,15,11,7,3,30,26,22,18,14,10,6,2,29,25,21,17,13,9,5,1,28,24..., dimensions={0} | all-to-all | bytes 163840 | tf_op jit(solution)/shard_map/all_to_all | solution.py:224
  16.5 1.8 %render.1 = f32[4,16,128]{2,1,0:T(8,128)} custom-call(s32[1]{0:T(128)S(6)} %copy.5.refs_0_, f32[8,128]{1,0:T(8,128)S(1)} %get-tuple-element.7.refs_1_, f32[160,128]{1,0:T(8,128)S(1)} %bitcast.4), custom_call_target="tpu_custom_call" | custom-call | tf_op jit(solution)/shard_map/render/pallas_call | solution.py:227

commit v15 on v14

--- a/solution.py
+++ b/solution.py
@@ -39,7 +39,7 @@
     _, columns, rows = coef_ref.shape
     strip = columns // tiles
     band = rows // depths
-    moves = ((coef_hbm, coef_ref), (keep_hbm, keep_ref))
+    moves = [(coef_hbm.at[pl.ds(k, 4)], coef_ref.at[pl.ds(k, 4)]) for k in (0, 4)] + [(keep_hbm, keep_ref)]
     fetches = [pltpu.make_async_copy(a, b, arrival.at[i]) for i, (a, b) in enumerate(moves)]
     for fetch in fetches:
         fetch.start()
@@ -83,7 +83,7 @@
             out_ref[listed_at(t, d, tiles, depths), :, 0, :] = rows_ref[d, :, t, :]
 
 
-def unpack(packed_ref, coef_ref):
+def unpack(packed_ref, coef_ref, scales):
     zblocks, lanes = packed_ref.shape[0] // 5, packed_ref.shape[1]
     first = lax.broadcasted_iota(jnp.int32, (zblocks, lanes), 1) < lanes // 2
     row = [packed_ref[pl.ds(q, zblocks, stride=5), :] for q in range(5)]
@@ -93,17 +93,17 @@
     slot.append(jnp.where(keep > 4, jnp.where(first, row[4], turned[4]), 0.0))
     slot += [jnp.where(keep > k, turned[8 - k], 0.0) for k in (5, 6, 7)]
     for k in range(8):
-        coef_ref[k] = slot[k]
+        coef_ref[k] = slot[k] * scales[k] if k in scales else slot[k]
 
 
 def render_kernel(
     flip_ref, sign_ref, packed_ref, out_hbm, coef_ref, out_ref, leaving, *, strip, band, samples
 ):
-    unpack(packed_ref, coef_ref)
     slots, zblocks, lanes = coef_ref.shape
     sign = sign_ref[...]
     flipped = flip_ref[0] > 0
     b1 = [cosine(1, i) for i in range(EDGE)]
+    unpack(packed_ref, coef_ref, {0: 0.125 * LOG2E, 3: 0.25 * LOG2E * b1[0] * sign[:1]})
     row = lax.broadcasted_iota(jnp.int32, (2 * EDGE, lanes), 0)
     y, x = split(row, EDGE)
 
@@ -117,17 +117,14 @@
     x2 = table(x, [cosine(2, i) for i in range(EDGE)])
     y1 = table(y, b1[:2])
     y2 = table(y, [cosine(2, i) for i in range(2)])
-    c_dc = 0.125 * LOG2E
     c_x1 = (0.25 * LOG2E) * x1
     c_x2 = (0.25 * LOG2E) * x2
     c_y1 = (0.25 * LOG2E) * y1
     c_y2 = (0.25 * LOG2E) * y2
     c_xy = (0.5 * LOG2E) * x1 * y1
-    c_z = jnp.full((2 * EDGE, lanes), 0.25 * LOG2E * b1[0], jnp.float32) * sign
     c_zy = (0.5 * LOG2E * b1[0]) * y1 * sign
     ratio = b1[1] / b1[0]
-    blue_one = 2.0**-20
-    blue_factor = blue_one * math.exp(-1.5)
+    blue_factor = math.exp(-1.5)
     fade = -1.5 / samples
 
     def block(step, state):
@@ -136,9 +133,9 @@
         a = [
             jnp.broadcast_to(coef_ref[k, pl.ds(zb, 1), :], (2 * EDGE, lanes)) for k in range(slots)
         ]
-        even = a[0] * c_dc + a[2] * c_x1 + a[4] * c_y2 + a[6] * c_x2
+        even = a[0] + a[2] * c_x1 + a[4] * c_y2 + a[6] * c_x2
         odd = a[1] * c_y1 + a[5] * c_xy
-        g_even = a[3] * c_z
+        g_even = a[3]
         g_odd = a[7] * c_zy
         halves = []
         for h in range(2):
@@ -153,11 +150,9 @@
                 after = jnp.exp2(fade * depth)
                 weight = before - after
                 before = after
-                blue_u = blue_one + blue_factor * v
-                shared = weight / (one_u * blue_u)
-                red = red + shared * blue_u
+                red = red + weight / one_u
                 green = green + weight * jnp.exp2(f * (f * (-1.0 / LOG2E)))
-                blue = blue + shared * one_u
+                blue = blue + weight / (1.0 + blue_factor * v)
             halves.append((depth, before, red, green, blue))
         return tuple(halves)
 
@@ -174,7 +169,7 @@
     outs = []
     for _, before, red, green, blue in state:
         opacity = 1.0 - before
-        outs.append((opacity - red, green, blue * blue_one, opacity))
+        outs.append((opacity - red, green, blue, opacity))
     copies = [pltpu.make_async_copy(out_ref.at[ch], out_hbm.at[ch], leaving.at[ch]) for ch in range(4)]
     for ch in range(4):
         for b in range(strip):
@@ -213,7 +208,7 @@
             pltpu.VMEM((slots, columns, rows), jnp.float32),
             pltpu.VMEM((columns, rows), jnp.int32),
             pltpu.VMEM((depths, 5, tiles, lanes), jnp.float32),
-            pltpu.SemaphoreType.DMA((2,)),
+            pltpu.SemaphoreType.DMA((3,)),
         ],
         compiler_params=params,
         name="pack",

time: 18.5 us -> 18.4 us (level)
  no operation moved by 1% of the time
where the time goes in v15:
time: 18.4 us; the launch traced here: 18.2 us
  blocking collectives  14.6 us (79%)
  Pallas kernels  2.99 us (16%)
  between operations  0.66 us (4%)
    all_to_all x1, blocking collectives, per_device(): lax.all_to_all(chunks, ('depth', 'tile'), split_axis=0, concat_axis=0, ti...  14.6 us
    pallas_call x1, Pallas kernels, per_device(): pl.pallas_call(lambda *refs: render_kernel(*refs, strip=strip, band=band,...  1.82 us
    pallas_call x1, Pallas kernels, per_device(): pl.pallas_call(lambda *refs: pack_kernel(*refs, tiles=tiles, depths=depth...  1.17 us

profile of v15, /device:TPU:0, one launch (start us, length us, event | category | flops | bytes accessed | tf_op | source)
XLA Modules:
  0.0 18.2 jit_solution(16045280645828123000)
XLA Ops:
  0.7 1.2 %pack.1 = (f32[32,5,1,128]{3,2,1,0:T(1,128)S(1)}, f32[8,128]{1,0:T(8,128)S(1)}) custom-call(s32[1]{0:T(128)S(6)} %copy.5.refs_0_, f32[8,32,128]{2,1,0:T(8,128)} %bitcast.6, s32[32,128]{1,0:T(8,128)} %bitcast.7), custom_call_target="tpu_custom_call" | custom-call | tf_op jit(solution)/shard_map/pack/pallas_call | solution.py:199
  1.8 14.6 %all_to_all.5 = f32[32,1,640]{2,1,0:T(1,128)S(1)} all-to-all(f32[32,1,640]{2,1,0:T(1,128)S(1)} %bitcast.5), channel_id=1, replica_groups={{31,27,23,19,15,11,7,3,30,26,22,18,14,10,6,2,29,25,21,17,13,9,5,1,28,24..., dimensions={0} | all-to-all | bytes 163840 | tf_op jit(solution)/shard_map/all_to_all | solution.py:219
  16.4 1.8 %render.1 = f32[4,16,128]{2,1,0:T(8,128)} custom-call(s32[1]{0:T(128)S(6)} %copy.5.refs_0_, f32[8,128]{1,0:T(8,128)S(1)} %get-tuple-element.7.refs_1_, f32[160,128]{1,0:T(8,128)S(1)} %bitcast.4), custom_call_target="tpu_custom_call" | custom-call | tf_op jit(solution)/shard_map/render/pallas_call | solution.py:222

commit v16 on v15

--- a/solution.py
+++ b/solution.py
@@ -43,8 +43,6 @@
     fetches = [pltpu.make_async_copy(a, b, arrival.at[i]) for i, (a, b) in enumerate(moves)]
     for fetch in fetches:
         fetch.start()
-    for fetch in fetches:
-        fetch.wait()
     lane = lax.broadcasted_iota(jnp.int32, (tiles, rows), 1)
     odd = split(lane, 2)[1]
     even = odd == 0
@@ -53,6 +51,15 @@
         return jnp.take_along_axis(values, index, axis=1)
 
     other = lane + 1 - 2 * odd
+    sign_ref[...] = jnp.full(sign_ref.shape, 1 - 2 * flip_ref[0], jnp.int32).astype(jnp.float32)
+    half = strip * band // 2
+    chunk, within = split(lane, band // 2)
+    parity, column = split(chunk, strip)
+    parity = split(parity, 2)[1]
+    source = within * 2 + parity
+    sources = [source + d * band for d in range(depths)]
+    for fetch in fetches:
+        fetch.wait()
     packed = []
     for b in range(strip):
         mine = pl.ds(b, tiles, stride=strip)
@@ -63,15 +70,9 @@
             result.append(jnp.where(keep > q, slot[q], take(slot[8 - q], other)))
         result[4] = jnp.where(even, result[4], (9 - keep).astype(jnp.float32))
         packed.append(result)
-    sign_ref[...] = jnp.full(sign_ref.shape, 1 - 2 * flip_ref[0], jnp.int32).astype(jnp.float32)
-    half = strip * band // 2
-    chunk, within = split(lane, band // 2)
-    parity, column = split(chunk, strip)
-    parity = split(parity, 2)[1]
-    source = within * 2 + parity
     for d in range(depths):
         for q in range(5):
-            gathered = [take(packed[b][q], source + d * band) for b in range(strip)]
+            gathered = [take(packed[b][q], sources[d]) for b in range(strip)]
             merged = gathered[0]
             for b in range(1, strip):
                 merged = jnp.where(column == b, gathered[b], merged)

time: 18.4 us -> 18.4 us (level)
  no operation moved by 1% of the time
where the time goes in v16:
time: 18.4 us; the launch traced here: 18.2 us
  blocking collectives  14.6 us (79%)
  Pallas kernels  2.98 us (16%)
  between operations  0.66 us (4%)
    all_to_all x1, blocking collectives, per_device(): lax.all_to_all(chunks, ('depth', 'tile'), split_axis=0, concat_axis=0, ti...  14.6 us
    pallas_call x1, Pallas kernels, per_device(): pl.pallas_call(lambda *refs: render_kernel(*refs, strip=strip, band=band,...  1.82 us
    pallas_call x1, Pallas kernels, per_device(): pl.pallas_call(lambda *refs: pack_kernel(*refs, tiles=tiles, depths=depth...  1.16 us

profile of v16, /device:TPU:0, one launch (start us, length us, event | category | flops | bytes accessed | tf_op | source)
XLA Modules:
  0.0 18.2 jit_solution(11742476877668268209)
XLA Ops:
  0.7 1.2 %pack.1 = (f32[32,5,1,128]{3,2,1,0:T(1,128)S(1)}, f32[8,128]{1,0:T(8,128)S(1)}) custom-call(s32[1]{0:T(128)S(6)} %copy.5.refs_0_, f32[8,32,128]{2,1,0:T(8,128)} %bitcast.6, s32[32,128]{1,0:T(8,128)} %bitcast.7), custom_call_target="tpu_custom_call" | custom-call | tf_op jit(solution)/shard_map/pack/pallas_call | solution.py:200
  1.8 14.6 %all_to_all.5 = f32[32,1,640]{2,1,0:T(1,128)S(1)} all-to-all(f32[32,1,640]{2,1,0:T(1,128)S(1)} %bitcast.5), channel_id=1, replica_groups={{31,27,23,19,15,11,7,3,30,26,22,18,14,10,6,2,29,25,21,17,13,9,5,1,28,24..., dimensions={0} | all-to-all | bytes 163840 | tf_op jit(solution)/shard_map/all_to_all | solution.py:220
  16.4 1.8 %render.1 = f32[4,16,128]{2,1,0:T(8,128)} custom-call(s32[1]{0:T(128)S(6)} %copy.5.refs_0_, f32[8,128]{1,0:T(8,128)S(1)} %get-tuple-element.7.refs_1_, f32[160,128]{1,0:T(8,128)S(1)} %bitcast.4), custom_call_target="tpu_custom_call" | custom-call | tf_op jit(solution)/shard_map/render/pallas_call | solution.py:223
